TPU v7x, 32 devices: a whole 2x2x4 slice. The times are simulated.
32 devices in a mesh: dp: 8 (over z, x), mp: 4 (over y, core).
Axes of the slice: x: 2, y: 2, z: 4, core: 2. Of those that a mesh axis runs over, the one named last changes fastest.
Arguments:
- block_input: bfloat16 [24576, 1024], P(('dp', 'mp')), may hold values from -6 to 6
- sequence_lengths: int32 [8, 6], P('dp'), may hold values from 0 to 1024, as said below
- first_gain: float32 [1024], replicated, may hold values from 0.5 to 1.5
- first_shift: float32 [1024], replicated, may hold values from -3 to 3
- second_gain: float32 [1024], replicated, may hold values from 0.5 to 1.5
- second_shift: float32 [1024], replicated, may hold values from -3 to 3
- triple_weight: bfloat16 [1024, 3072], P(None, 'mp'), may hold values from -0.1875 to 0.1875
- triple_left: bfloat16 [1024, 128], replicated, may hold values from -0.1875 to 0.1875
- triple_right: bfloat16 [128, 3072], replicated, may hold values from -0.25 to 0.25
- output_weight: bfloat16 [1024, 1024], P('mp'), may hold values from -0.5 to 0.5
- output_left: bfloat16 [1024, 128], replicated, may hold values from -0.5 to 0.5
- output_right: bfloat16 [128, 1024], replicated, may hold values from -0.25 to 0.25
- expand_weight: bfloat16 [1024, 4096], P(None, 'mp'), may hold values from -0.1875 to 0.1875
- expand_left: bfloat16 [1024, 128], replicated, may hold values from -0.1875 to 0.1875
- expand_right: bfloat16 [128, 4096], replicated, may hold values from -0.25 to 0.25
- shrink_weight: bfloat16 [4096, 1024], P('mp'), may hold values from -0.09375 to 0.09375
- shrink_left: bfloat16 [4096, 128], replicated, may hold values from -0.09375 to 0.09375
- shrink_right: bfloat16 [128, 1024], replicated, may hold values from -0.25 to 0.25
- cotangent: bfloat16 [24576, 1024], P(('dp', 'mp')), may hold values from -6 to 6
Outputs:
- block_output: bfloat16 [24576, 1024], P(('dp', 'mp'))
- input_gradient: float32 [24576, 1024], P(('dp', 'mp'))
- first_gain_gradient: float32 [1024], replicated
- first_shift_gradient: float32 [1024], replicated
- second_gain_gradient: float32 [1024], replicated
- second_shift_gradient: float32 [1024], replicated
- triple_left_gradient: float32 [1024, 128], replicated
- triple_right_gradient: float32 [128, 3072], replicated
- output_left_gradient: float32 [1024, 128], replicated
- output_right_gradient: float32 [128, 1024], replicated
- expand_left_gradient: float32 [1024, 128], replicated
- expand_right_gradient: float32 [128, 4096], replicated
- shrink_left_gradient: float32 [4096, 128], replicated
- shrink_right_gradient: float32 [128, 1024], replicated
Inputs may be any that keep to these rules, and one draw needn't show every extreme that they name: `sequence_lengths`: row g lists the lengths of the sequences of group g in order, each 512 or 1024, then zeros; every row sums to 3072 and holds at least one sequence of 1024.
All inputs are finite; a program needn't handle non-finite values.
Results may differ from a plain program's by a relative error of at most 0.012.
The roundings to bfloat16 on the way count: a program that leaves them out, or rounds other values in their place, can miss the bound.
Values may be sent and summed in bfloat16 or wider, within the bound.
A program may use at most 256 MiB of HBM per device.

v0:
```python
import functools
import math

import jax
import jax.numpy as jnp
import numpy as np
from jax import lax
from jax.experimental import pallas as pl
from jax.experimental.pallas import tpu as pltpu
from jax.sharding import PartitionSpec as P

HEAD_DIM = 64
ROT = 16
SHORT = 512
TOK_GRP = 3072
SLOTS = 6
EPS = 1e-05
LANES = 128
MESH = pl.DeviceIdType.MESH
BF16 = jnp.bfloat16
F32 = jnp.float32
VMEM_LIMIT = 56 * 1024 * 1024
BRIEF = pl.CostEstimate(flops=1, bytes_accessed=1, transcendentals=0)


def dot_nn(former, latter):
    return lax.dot_general(
        former, latter, (((1,), (0,)), ((), ())), preferred_element_type=F32
    )


def dot_nt(former, latter):
    return lax.dot_general(
        former, latter, (((1,), (1,)), ((), ())), preferred_element_type=F32
    )


def dot_tn(former, latter):
    return lax.dot_general(
        former, latter, (((0,), (0,)), ((), ())), preferred_element_type=F32
    )


def find_flags(group_lengths):
    seq_ends = jnp.cumsum(group_lengths, dtype=jnp.int32)
    starts = seq_ends - group_lengths
    block_starts = jnp.arange(SLOTS, dtype=jnp.int32) * SHORT
    begins = jnp.any(
        (starts[None, :] == block_starts[:, None]) & (group_lengths[None, :] > 0), axis=1
    )
    return jnp.where(begins, 0, 1).astype(jnp.int32)


def rotary_tables():
    half = ROT // 2
    frequency = np.exp(
        np.arange(half, dtype=np.float32) * np.float32(-2.0 * math.log(10000.0) / ROT)
    ).astype(np.float32)
    angles = np.arange(2 * SHORT, dtype=np.float32)[:, None] * frequency[None, :]
    cosine = np.ones((2 * SHORT, LANES), np.float32)
    minus = np.zeros((2 * SHORT, LANES), np.float32)
    plus = np.zeros((2 * SHORT, LANES), np.float32)
    for base in range(0, LANES, HEAD_DIM):
        cosine[:, base : base + half] = np.cos(angles)
        cosine[:, base + half : base + ROT] = np.cos(angles)
        minus[:, base : base + half] = -np.sin(angles)
        plus[:, base + half : base + ROT] = np.sin(angles)
    return jnp.asarray(cosine), jnp.asarray(minus), jnp.asarray(plus)


def low_lanes():
    return lax.broadcasted_iota(jnp.int32, (1, LANES), 1) < HEAD_DIM


def rotate(pair, cosine, minus, plus):
    half = ROT // 2
    return (
        pair * cosine
        + pltpu.roll(pair, LANES - half, 1) * minus
        + pltpu.roll(pair, half, 1) * plus
    )


def unrotate(pair, cosine, minus, plus):
    half = ROT // 2
    return (
        pair * cosine
        - pltpu.roll(pair, LANES - half, 1) * minus
        - pltpu.roll(pair, half, 1) * plus
    )


def normalize(values, gain, shift):
    center = values - jnp.mean(values, axis=-1, keepdims=True)
    spread = jnp.mean(center * center, axis=-1, keepdims=True)
    return center * lax.rsqrt(spread + EPS) * gain + shift


def whole(shape):
    return pl.BlockSpec(
        shape, lambda *idx: (0,) * len(shape), pipeline_mode=pl.Buffered(1)
    )


def held(shape):
    return pl.BlockSpec(shape, lambda *idx: (0,) * len(shape))


def rows_of(tile, width):
    return pl.BlockSpec((tile, width), lambda i, *refs: (i, 0))


def shaped(shape, dtype):
    return jax.ShapeDtypeStruct(shape, dtype)


def params(semantics=1):
    return pltpu.CompilerParams(
        dimension_semantics=("arbitrary",) * semantics, vmem_limit_bytes=VMEM_LIMIT
    )


def unit_gather_kernel(unit, x_ref, d_ref, xg_ref, dg_ref, local_sem, send_sem, recv_sem):
    dp = lax.axis_index("dp")
    mp = lax.axis_index("mp")
    place = lax.rem(mp, unit)
    base = mp - place
    peers = [(dp, base + lax.rem(place + j, unit)) for j in range(1, unit)]
    barrier = pltpu.get_barrier_semaphore()
    for peer in peers:
        pl.semaphore_signal(barrier, inc=1, device_id=peer, device_id_type=MESH)
    pl.semaphore_wait(barrier, unit - 1)
    rows = x_ref.shape[0]
    span = pl.ds(pl.multiple_of(place * rows, rows), rows)
    copies = []
    for which, (src, dst) in enumerate(((x_ref, xg_ref), (d_ref, dg_ref))):
        for j, peer in enumerate(peers):
            copies.append(
                pltpu.make_async_remote_copy(
                    src_ref=src,
                    dst_ref=dst.at[span],
                    send_sem=send_sem.at[which, j],
                    recv_sem=recv_sem.at[which, j],
                    device_id=peer,
                    device_id_type=MESH,
                )
            )
        copies.append(pltpu.make_async_copy(src, dst.at[span], local_sem.at[which]))
    for copy in copies:
        copy.start()
    for copy in copies:
        copy.wait()


def unit_gather(unit, x, d):
    rows, width = x.shape
    anywhere = pl.BlockSpec(memory_space=pl.ANY)
    return pl.pallas_call(
        functools.partial(unit_gather_kernel, unit),
        out_shape=[shaped((rows * unit, width), x.dtype)] * 2,
        in_specs=[pl.BlockSpec(memory_space=pltpu.VMEM)] * 2,
        out_specs=[anywhere] * 2,
        scratch_shapes=[
            pltpu.SemaphoreType.DMA((2,)),
            pltpu.SemaphoreType.DMA((2, unit - 1)),
            pltpu.SemaphoreType.DMA((2, unit - 1)),
        ],
        compiler_params=pltpu.CompilerParams(
            collective_id=1, has_side_effects=True, vmem_limit_bytes=VMEM_LIMIT
        ),
        cost_estimate=BRIEF,
        name="unit_gather",
    )(x, d)


def gelu_parts(hidden):
    cdf = 0.5 + 0.5 * lax.erf(hidden * math.sqrt(0.5))
    density = jnp.exp(-0.5 * hidden * hidden) * (1.0 / math.sqrt(2.0 * math.pi))
    return hidden * cdf, cdf + hidden * density


def feed_core(
    normed, low, dy, grad_low, up_ref, up_right_ref, down_ref, down_left_ref, act_ref, grad_ref, hidden_step
):
    hidden_width = up_ref.shape[1]
    for start in range(0, hidden_width, hidden_step):
        cols = pl.ds(start, hidden_step)
        hidden = dot_nn(normed, up_ref[:, cols]) + dot_nn(low, up_right_ref[:, cols])
        grad_act = dot_nt(dy, down_ref[cols, :]) + dot_nt(grad_low, down_left_ref[cols, :])
        activated, slope = gelu_parts(hidden)
        act_ref[:, cols] = activated.astype(BF16)
        grad_ref[:, cols] = (grad_act * slope).astype(BF16)


def chip_neighbours(unit):
    dp = lax.axis_index("dp")
    mp = lax.axis_index("mp")
    lead = lax.rem(dp, 2)
    return lead, (dp, lax.rem(mp + unit, 2 * unit)), (dp + 1 - 2 * lead, mp)


def courier(unit, pairs, chunks, y_sems, x_sems):
    lead, y_peer, x_peer = chip_neighbours(unit)
    over_y, over_x = [], []
    for k in range(chunks):
        for j, (own, far) in enumerate(pairs):
            count = own.shape[0] // 2 // chunks
            span = pl.ds(pl.multiple_of((lead * chunks + k) * count, count), count)
            for src, sems, peer, group in ((own, y_sems, y_peer, over_y), (far, x_sems, x_peer, over_x)):
                group.append(
                    pltpu.make_async_remote_copy(
                        src_ref=src.at[span],
                        dst_ref=far.at[span],
                        send_sem=sems.at[0, k, j],
                        recv_sem=sems.at[1, k, j],
                        device_id=peer,
                        device_id_type=MESH,
                    )
                )
    return over_y, over_x


def meet(peers):
    barrier = pltpu.get_barrier_semaphore()
    for peer in peers:
        pl.semaphore_signal(barrier, inc=1, device_id=peer, device_id_type=MESH)
    pl.semaphore_wait(barrier, len(peers))


def feed_first_kernel(
    unit, steps, x_ref, dy_ref, gain_ref, shift_ref, up_ref, up_left_ref, up_right_ref, down_ref, down_left_ref,
    output_right_ref, down_right_ref, triple_ref, output_ref, normed_ref, low_ref, grad_lows_ref, out_ref, grad_ref,
    low_act_ref, grad_low_ref, up_right_grad_ref, down_left_grad_ref, triple_far_ref, output_far_ref, act_ref, gh_ref,
    y_sems, x_sems,
):
    step = pl.program_id(0)
    chunks = y_sems.shape[1]
    over_y, over_x = courier(
        unit, ((triple_ref, triple_far_ref), (output_ref, output_far_ref)), chunks, y_sems, x_sems
    )

    @pl.when(step == 0)
    def _():
        meet(chip_neighbours(unit)[1:])
        for copy in over_y:
            copy.start()

    for k in range(chunks):

        @pl.when(step == min(k + 1, steps - 1))
        def _():
            for j in (2 * k, 2 * k + 1):
                over_y[j].wait_recv()
                over_x[j].start()

    normed = normalize(x_ref[...].astype(F32), gain_ref[...], shift_ref[...]).astype(BF16)
    normed_ref[...] = normed
    dy = dy_ref[...]
    low = dot_nn(normed, up_left_ref[...]).astype(BF16)
    low_ref[...] = low
    rights = jnp.concatenate([output_right_ref[...], down_right_ref[...]], axis=0)
    grad_lows = dot_nt(dy, rights).astype(BF16)
    grad_lows_ref[...] = grad_lows
    grad_low = grad_lows[:, LANES:]
    feed_core(normed, low, dy, grad_low, up_ref, up_right_ref, down_ref, down_left_ref, act_ref, gh_ref, 256)
    act = act_ref[...]
    gh = gh_ref[...]
    out_ref[...] = dot_nn(act, down_ref[...])
    grad_ref[...] = dot_nt(gh, up_ref[...])
    low_act_ref[...] = dot_nn(act, down_left_ref[...])
    grad_low_ref[...] = dot_nt(gh, up_right_ref[...])

    @pl.when(pl.program_id(0) == 0)
    def _():
        up_right_grad_ref[...] = jnp.zeros_like(up_right_grad_ref)
        down_left_grad_ref[...] = jnp.zeros_like(down_left_grad_ref)

    up_right_grad_ref[...] += dot_tn(low, gh)
    down_left_grad_ref[...] += dot_tn(grad_low, act)

    @pl.when(step == steps - 1)
    def _():
        for copy in over_y:
            copy.wait_send()
        for copy in over_x:
            copy.wait()


def at_columns(shape, which):
    return pl.BlockSpec(shape, lambda i, meta: (0, meta[which]), pipeline_mode=pl.Buffered(1))


def at_rows(shape, which):
    return pl.BlockSpec(shape, lambda i, meta: (meta[which], 0), pipeline_mode=pl.Buffered(1))


OWN, FAR, LEAD, PLACE, CONT = 0, 1, 2, 3, 4


def feed_first(unit, x, dy, gain, shift, up, up_left, up_right, down, down_left, output_right, down_right, triple,
               output, tile):
    rows, width = x.shape
    hidden = up.shape[1]
    steps = rows // tile
    chunks = math.gcd(4, output.shape[0] // 32)
    anywhere = pl.BlockSpec(memory_space=pl.ANY)
    return pl.pallas_call(
        functools.partial(feed_first_kernel, unit, steps),
        grid=(steps,),
        in_specs=[
            rows_of(tile, width),
            rows_of(tile, width),
            whole((1, width)),
            whole((1, width)),
            whole(up.shape),
            whole(up_left.shape),
            pl.BlockSpec((LANES, hidden), lambda i: (0, lax.axis_index("mp")), pipeline_mode=pl.Buffered(1)),
            whole(down.shape),
            pl.BlockSpec((hidden, LANES), lambda i: (lax.axis_index("mp"), 0), pipeline_mode=pl.Buffered(1)),
            whole(output_right.shape),
            whole(down_right.shape),
            anywhere,
            anywhere,
        ],
        out_specs=[
            rows_of(tile, width),
            rows_of(tile, LANES),
            rows_of(tile, 2 * LANES),
            rows_of(tile, width),
            rows_of(tile, width),
            rows_of(tile, LANES),
            rows_of(tile, LANES),
            held((LANES, hidden)),
            held((LANES, hidden)),
            anywhere,
            anywhere,
        ],
        scratch_shapes=[
            pltpu.VMEM((tile, hidden), BF16),
            pltpu.VMEM((tile, hidden), BF16),
            pltpu.SemaphoreType.DMA((2, chunks, 2)),
            pltpu.SemaphoreType.DMA((2, chunks, 2)),
        ],
        out_shape=[
            shaped((rows, width), BF16),
            shaped((rows, LANES), BF16),
            shaped((rows, 2 * LANES), BF16),
            shaped((rows, width), F32),
            shaped((rows, width), F32),
            shaped((rows, LANES), F32),
            shaped((rows, LANES), F32),
            shaped((LANES, hidden), F32),
            shaped((LANES, hidden), F32),
            shaped(triple.shape, BF16),
            shaped(output.shape, BF16),
        ],
        compiler_params=pltpu.CompilerParams(
            dimension_semantics=("arbitrary",), vmem_limit_bytes=VMEM_LIMIT, collective_id=3, has_side_effects=True
        ),
        cost_estimate=BRIEF,
        name="feed_first",
    )(x, dy, gain, shift, up, up_left, up_right, down, down_left, output_right, down_right, triple, output)


def join_halves(step, lead, pieces, whole_ref):
    @pl.when(step == 0)
    def _():
        count = pieces[0].shape[0]
        for j, piece in enumerate(pieces):
            place = j + lead * (1 - 2 * j)
            whole_ref[pl.ds(pl.multiple_of(place * count, count), count), :] = piece[...]


def feed_second_kernel(
    send_tiles, meta_ref, normed_ref, low_ref, dy_ref, grad_lows_ref, out_in_ref, grad_in_ref, low_act_in_ref,
    grad_low_in_ref, up0_ref, up1_ref, up_left_ref, up_right_ref, down0_ref, down1_ref, down_left_ref, send_ref,
    keep_ref, up_right_grad_ref, down_left_grad_ref, up_left_grad_ref, act_ref, gh_ref, up_ref, down_ref,
):
    step = pl.program_id(0)
    join_halves(step, meta_ref[LEAD], (up0_ref, up1_ref), up_ref)
    join_halves(step, meta_ref[LEAD], (down0_ref, down1_ref), down_ref)
    normed = normed_ref[...]
    low = low_ref[...]
    dy = dy_ref[...]
    grad_low = grad_lows_ref[:, LANES:]
    feed_core(normed, low, dy, grad_low, up_ref, up_right_ref, down_ref, down_left_ref, act_ref, gh_ref, 256)
    act = act_ref[...]
    gh = gh_ref[...]
    grad_low_up = (grad_low_in_ref[...] + dot_nt(gh, up_right_ref[...])).astype(BF16)
    out = (out_in_ref[...] + dot_nn(act, down_ref[...])).astype(BF16)
    low_act = (low_act_in_ref[...] + dot_nn(act, down_left_ref[...])).astype(BF16)
    grad = (
        grad_in_ref[...] + dot_nt(gh, up_ref[...]) + dot_nt(grad_low_up, up_left_ref[...])
    ).astype(BF16)
    width = out.shape[1]

    def put(ref):
        ref[:, :width] = out
        ref[:, width : 2 * width] = grad
        ref[:, 2 * width :] = low_act

    pl.when(step < send_tiles)(lambda: put(send_ref))
    pl.when(step >= send_tiles)(lambda: put(keep_ref))

    @pl.when(step == 0)
    def _():
        up_right_grad_ref[...] = jnp.zeros_like(up_right_grad_ref)
        down_left_grad_ref[...] = jnp.zeros_like(down_left_grad_ref)
        up_left_grad_ref[...] = jnp.zeros_like(up_left_grad_ref)

    up_right_grad_ref[...] += dot_tn(low, gh)
    down_left_grad_ref[...] += dot_tn(grad_low, act)
    up_left_grad_ref[...] += dot_tn(grad_low_up, normed)


def ordered(tile, width, tiles, per_device):
    return pl.BlockSpec(
        (tile, width), lambda i, meta: (lax.rem(i + (meta[PLACE] + 1) * per_device, tiles), 0)
    )


def sent(tile, width, tiles):
    return pl.BlockSpec((tile, width), lambda i, meta: (jnp.minimum(i, tiles - 1), 0))


def kept(tile, width, tiles):
    return pl.BlockSpec((tile, width), lambda i, meta: (jnp.maximum(i - tiles, 0), 0))


def feed_second(meta, normed, low, dy, grad_lows, out, grad, low_act, grad_low, ups, up_left, up_right, downs,
                down_left, own_rows, tile):
    rows, width = normed.shape
    hidden = ups[0].shape[1]
    send_rows = rows - own_rows
    tiles = send_rows // tile
    row_spec = functools.partial(ordered, tiles=rows // tile, per_device=own_rows // tile)
    wide = 2 * width + LANES
    return pl.pallas_call(
        functools.partial(feed_second_kernel, tiles),
        grid_spec=pltpu.PrefetchScalarGridSpec(
            num_scalar_prefetch=1,
            grid=(rows // tile,),
            in_specs=[
                row_spec(tile, width),
                row_spec(tile, LANES),
                row_spec(tile, width),
                row_spec(tile, 2 * LANES),
                row_spec(tile, width),
                row_spec(tile, width),
                row_spec(tile, LANES),
                row_spec(tile, LANES),
                whole(ups[0].shape),
                whole(ups[1].shape),
                whole(up_left.shape),
                at_columns((LANES, hidden), FAR),
                whole(downs[0].shape),
                whole(downs[1].shape),
                at_rows((hidden, LANES), FAR),
            ],
            out_specs=[
                sent(tile, wide, tiles),
                kept(tile, wide, tiles),
                held((LANES, hidden)),
                held((LANES, hidden)),
                held((LANES, width)),
            ],
            scratch_shapes=[
                pltpu.VMEM((tile, hidden), BF16),
                pltpu.VMEM((tile, hidden), BF16),
                pltpu.VMEM((width, hidden), BF16),
                pltpu.VMEM((hidden, width), BF16),
            ],
        ),
        out_shape=[
            shaped((send_rows, wide), BF16),
            shaped((own_rows, wide), BF16),
            shaped((LANES, hidden), F32),
            shaped((LANES, hidden), F32),
            shaped((LANES, width), F32),
        ],
        compiler_params=params(),
        cost_estimate=BRIEF,
        name="feed_second",
    )(meta, normed, low, dy, grad_lows, out, grad, low_act, grad_low, *ups, up_left, up_right, *downs, down_left)


def project_kernel(
    halo_tiles, meta_ref, x_halo_ref, x_ref, dy_ref, grad_lows_ref, gain_ref, shift_ref, triple0_ref, triple1_ref,
    left_ref, right0_ref, right1_ref, output0_ref, output1_ref, output_left0_ref, output_left1_ref, cos_ref,
    minus_ref, plus_ref, normed_ref, low_ref, q_ref, k_ref, v_ref, g_ref,
):
    step = pl.program_id(0)
    tables = (cos_ref[...], minus_ref[...], plus_ref[...])
    head_width = output0_ref.shape[0]
    first = low_lanes()

    def rows(x, full):
        normed = normalize(x.astype(F32), gain_ref[...], shift_ref[...]).astype(BF16)
        low = dot_nn(normed, left_ref[...]).astype(BF16)
        if full:
            normed_ref[...] = normed
            low_ref[...] = low
        for shard, (triple, right) in enumerate(((triple0_ref, right0_ref), (triple1_ref, right1_ref))):
            mixed = dot_nn(normed, triple[...]) + dot_nn(low, right[...])
            for pair in range(head_width // LANES):
                one, two, three = (
                    mixed[:, (3 * pair + part) * LANES : (3 * pair + part + 1) * LANES] for part in range(3)
                )
                cols = pl.ds(shard * head_width + pair * LANES, LANES)
                key = pltpu.roll(jnp.where(first, three, one), HEAD_DIM, 1)
                k_ref[:, cols] = rotate(key, *tables).astype(BF16)
                v_ref[:, cols] = jnp.where(first, two, three).astype(BF16)
                if full:
                    query = rotate(jnp.where(first, one, two), *tables).astype(BF16)
                    q_ref[:, cols] = query * HEAD_DIM**-0.5

    @pl.when(step < halo_tiles)
    def _():
        rows(x_halo_ref[...], False)

    @pl.when(step >= halo_tiles)
    def _():
        rows(x_ref[...], True)
        dy = dy_ref[...]
        grad_low = grad_lows_ref[:, :LANES]
        outputs = jnp.concatenate([output0_ref[...], output1_ref[...]], axis=0)
        lefts = jnp.concatenate([output_left0_ref[...], output_left1_ref[...]], axis=0)
        g_ref[...] = (dot_nt(dy, outputs) + dot_nt(grad_low, lefts)).astype(BF16)


def project(meta, x_halo, x, dy, grad_lows, gain, shift, triples, left, right, outputs, output_left, tables, tile):
    rows, width = dy.shape
    head_width = outputs[0].shape[0]
    triple_width = triples[0].shape[1]
    per_block = SHORT // tile
    halo_tiles = SHORT // tile

    def table_index(i, meta):
        j = jnp.maximum(i - halo_tiles, 0)
        block = meta[CONT + j // per_block] * per_block + lax.rem(j, per_block)
        return (jnp.where(i < halo_tiles, i, block), 0)

    table = pl.BlockSpec((tile, LANES), table_index)

    def main(size):
        return pl.BlockSpec((tile, size), lambda i, meta: (jnp.maximum(i - halo_tiles, 0), 0))

    return pl.pallas_call(
        functools.partial(project_kernel, halo_tiles),
        grid_spec=pltpu.PrefetchScalarGridSpec(
            num_scalar_prefetch=1,
            grid=(halo_tiles + rows // tile,),
            in_specs=[
                pl.BlockSpec((tile, width), lambda i, meta: (jnp.minimum(i, halo_tiles - 1), 0)),
                main(width),
                main(width),
                main(2 * LANES),
                whole(gain.shape),
                whole(shift.shape),
                whole(triples[0].shape),
                whole(triples[1].shape),
                whole(left.shape),
                at_columns((LANES, triple_width), OWN),
                at_columns((LANES, triple_width), FAR),
                whole(outputs[0].shape),
                whole(outputs[1].shape),
                at_rows((head_width, LANES), OWN),
                at_rows((head_width, LANES), FAR),
                table,
                table,
                table,
            ],
            out_specs=[
                main(width),
                main(LANES),
                main(2 * head_width),
                rows_of(tile, 2 * head_width),
                rows_of(tile, 2 * head_width),
                main(2 * head_width),
            ],
        ),
        out_shape=[
            shaped((rows, width), BF16),
            shaped((rows, LANES), BF16),
            shaped((rows, 2 * head_width), BF16),
            shaped((SHORT + rows, 2 * head_width), BF16),
            shaped((SHORT + rows, 2 * head_width), BF16),
            shaped((rows, 2 * head_width), BF16),
        ],
        compiler_params=params(),
        cost_estimate=BRIEF,
        name="project",
    )(meta, x_halo, x, dy, grad_lows, gain, shift, *triples, left, right, right, *outputs, output_left, output_left,
      *tables)


def attend_rows(with_prev, start, count, q_ref, k_ref, v_ref, g_ref, kp_ref, vp_ref, tables, att_ref, gq_ref,
                dk_ref, dv_ref, dkp_ref, dvp_ref):
    first_head = low_lanes()
    span = pl.ds(start, count)
    known = start + count
    zero = jnp.zeros((), BF16)

    def stack(pair):
        return jnp.concatenate([jnp.where(first_head, pair, zero), jnp.where(first_head, zero, pair)], axis=0)

    def unstack(both):
        return jnp.where(first_head, both[:count], both[count:])

    queries = stack(q_ref[span, :])
    grads = stack(g_ref[span, :])
    keys = k_ref[pl.ds(0, known), :]
    values = v_ref[pl.ds(0, known), :]
    scores = dot_nt(queries, keys)
    row = lax.broadcasted_iota(jnp.int32, (2 * count, known), 0)
    column = lax.broadcasted_iota(jnp.int32, (2 * count, known), 1)
    row = jnp.where(row >= count, row - count, row) + start
    scores = jnp.where(column <= row, scores, -1e30)
    peak = jnp.max(scores, axis=1, keepdims=True)
    if with_prev:
        prev_scores = dot_nt(queries, kp_ref[...])
        peak = jnp.maximum(peak, jnp.max(prev_scores, axis=1, keepdims=True))
        prev_exp = jnp.exp(prev_scores - peak)
    exp = jnp.exp(scores - peak)
    total = jnp.sum(exp, axis=1, keepdims=True)
    if with_prev:
        total = total + jnp.sum(prev_exp, axis=1, keepdims=True)
    scale = 1.0 / total
    weights = exp * scale
    weights_low = weights.astype(BF16)
    attended = dot_nn(weights_low, values)
    grad_weights = dot_nt(grads, values)
    inner = jnp.sum(weights * grad_weights, axis=1, keepdims=True)
    if with_prev:
        prev_weights = prev_exp * scale
        prev_low = prev_weights.astype(BF16)
        attended = attended + dot_nn(prev_low, vp_ref[...])
        prev_grad = dot_nt(grads, vp_ref[...])
        inner = inner + jnp.sum(prev_weights * prev_grad, axis=1, keepdims=True)
        prev_ds = (prev_weights * (prev_grad - inner)).astype(BF16)
    ds = (weights * (grad_weights - inner)).astype(BF16)
    grad_query = dot_nn(ds, keys)
    if with_prev:
        grad_query = grad_query + dot_nn(prev_ds, kp_ref[...])
        dkp_ref[...] += dot_tn(prev_ds, queries)
        dvp_ref[...] += dot_tn(prev_low, grads)
    dk_ref[pl.ds(0, known), :] += dot_tn(ds, queries)
    dv_ref[pl.ds(0, known), :] += dot_tn(weights_low, grads)
    att_ref[span, :] = unstack(attended).astype(BF16)
    grad_query = unstack(grad_query) * HEAD_DIM**-0.5
    gq_ref[span, :] = unrotate(grad_query, *[table[start : start + count] for table in tables]).astype(BF16)


def attend_kernel(
    blocks, count, meta_ref, q_ref, k_ref, v_ref, g_ref, kp_ref, vp_ref, cos_ref, minus_ref, plus_ref, att_ref, gq_ref,
    gk_ref, gv_ref, halo_ref, dk_ref, dv_ref, dkp_ref, dvp_ref,
):
    step = pl.program_id(1)
    block = blocks - 1 - step
    continued = meta_ref[CONT + block]
    offset = pl.multiple_of(continued * SHORT, SHORT)
    tables = tuple(ref[pl.ds(offset, SHORT), :] for ref in (cos_ref, minus_ref, plus_ref))

    @pl.when(step == 0)
    def _():
        dk_ref[...] = jnp.zeros_like(dk_ref)
        dv_ref[...] = jnp.zeros_like(dv_ref)

    @pl.when(step > 0)
    def _():
        dk_ref[...] = dkp_ref[...]
        dv_ref[...] = dvp_ref[...]

    dkp_ref[...] = jnp.zeros_like(dkp_ref)
    dvp_ref[...] = jnp.zeros_like(dvp_ref)
    args = (q_ref, k_ref, v_ref, g_ref, kp_ref, vp_ref, tables, att_ref, gq_ref, dk_ref, dv_ref, dkp_ref, dvp_ref)

    @pl.when(continued == 0)
    def _():
        for start in range(0, SHORT, count):
            attend_rows(False, start, count, *args)

    @pl.when(continued != 0)
    def _():
        for start in range(0, SHORT, count):
            attend_rows(True, start, count, *args)

    gk_ref[...] = pltpu.roll(unrotate(dk_ref[...], *tables), HEAD_DIM, 1).astype(BF16)
    gv_ref[...] = dv_ref[...].astype(BF16)

    @pl.when(block == 0)
    def _():
        base = tuple(ref[pl.ds(0, SHORT), :] for ref in (cos_ref, minus_ref, plus_ref))
        halo_ref[0] = pltpu.roll(unrotate(dkp_ref[...], *base), HEAD_DIM, 1).astype(BF16)
        halo_ref[1] = dvp_ref[...].astype(BF16)


def attend(shard, meta, q, k, v, g, tables, count):
    rows, head_width = q.shape[0], q.shape[1] // 2
    blocks, pairs = rows // SHORT, head_width // LANES
    here = pl.BlockSpec((SHORT, LANES), lambda p, i, meta: (blocks - 1 - i, p + shard * pairs))
    after = pl.BlockSpec((SHORT, LANES), lambda p, i, meta: (blocks - i, p + shard * pairs))
    new = pl.BlockSpec((SHORT, LANES), lambda p, i, meta: (blocks - 1 - i, p))
    return pl.pallas_call(
        functools.partial(attend_kernel, blocks, count),
        grid_spec=pltpu.PrefetchScalarGridSpec(
            num_scalar_prefetch=1,
            grid=(pairs, blocks),
            in_specs=[here, after, after, here, here, here] + [whole(table.shape) for table in tables],
            out_specs=[new] * 4 + [pl.BlockSpec((2, SHORT, LANES), lambda p, i, meta: (0, 0, p))],
            scratch_shapes=[pltpu.VMEM((SHORT, LANES), F32)] * 4,
        ),
        out_shape=[shaped((rows, head_width), BF16)] * 4 + [shaped((2, SHORT, head_width), BF16)],
        compiler_params=params(2),
        cost_estimate=BRIEF,
        name="attend",
    )(meta, q, k, v, g, k, v, *tables)


def settle_kernel(
    send_tiles, halo_start, tiles, per_device, meta_ref, normed_ref, low_ref, grad_lows_ref, out_in_ref,
    att0_ref, att1_ref, gq0_ref, gq1_ref, gk0_ref, gk1_ref, gv0_ref, gv1_ref, halo0_ref, halo1_ref,
    triple0_ref, triple1_ref, left_ref, output0_ref, output1_ref, right0_ref, right1_ref, output_left0_ref,
    output_left1_ref, out_ref, send_ref, keep_ref, right_grad0_ref, right_grad1_ref, left_grad_ref,
    output_left_grad0_ref, output_left_grad1_ref,
):
    step = pl.program_id(0)
    here = (lax.rem(step + (meta_ref[PLACE] + 1) * per_device, tiles) >= halo_start).astype(F32)
    normed = normed_ref[...]
    low = low_ref[...]
    grad_low_out = grad_lows_ref[:, :LANES]
    att0, att1 = att0_ref[...], att1_ref[...]
    first = low_lanes()

    def mixed(gq, gk, gv, halo):
        key = (gk[...].astype(F32) + here * halo[0].astype(F32)).astype(BF16)
        value = (gv[...].astype(F32) + here * halo[1].astype(F32)).astype(BF16)
        query = gq[...]
        groups = []
        for start in range(0, query.shape[1], LANES):
            q, k, v = (part[:, start : start + LANES] for part in (query, key, value))
            groups += [jnp.where(first, q, k), jnp.where(first, v, q), jnp.where(first, k, v)]
        return jnp.concatenate(groups, axis=1)

    grad0 = mixed(gq0_ref, gk0_ref, gv0_ref, halo0_ref)
    grad1 = mixed(gq1_ref, gk1_ref, gv1_ref, halo1_ref)
    grad_low = (dot_nt(grad0, right0_ref[...]) + dot_nt(grad1, right1_ref[...])).astype(BF16)
    grad = (
        dot_nt(grad0, triple0_ref[...]) + dot_nt(grad1, triple1_ref[...]) + dot_nt(grad_low, left_ref[...])
    ).astype(BF16)
    out_ref[...] = out_in_ref[...] + dot_nn(att0, output0_ref[...]) + dot_nn(att1, output1_ref[...])
    low_att = (dot_nn(att0, output_left0_ref[...]) + dot_nn(att1, output_left1_ref[...])).astype(BF16)
    width = grad.shape[1]

    def put(ref):
        ref[:, :width] = grad
        ref[:, width:] = low_att

    pl.when(step < send_tiles)(lambda: put(send_ref))
    pl.when(step >= send_tiles)(lambda: put(keep_ref))
    sums = (right_grad0_ref, right_grad1_ref, left_grad_ref, output_left_grad0_ref, output_left_grad1_ref)

    @pl.when(step == 0)
    def _():
        for ref in sums:
            ref[...] = jnp.zeros_like(ref)

    right_grad0_ref[...] += dot_tn(low, grad0)
    right_grad1_ref[...] += dot_tn(low, grad1)
    left_grad_ref[...] += dot_tn(grad_low, normed)
    output_left_grad0_ref[...] += dot_tn(grad_low_out, att0)
    output_left_grad1_ref[...] += dot_tn(grad_low_out, att1)


def settle(meta, normed, low, grad_lows, out, pairs, halos, triples, left, outputs, right, output_left, own_rows, tile):
    rows, width = normed.shape
    head_width = pairs[0].shape[1]
    send_rows = rows - own_rows
    send_tiles, tiles, per_device = send_rows // tile, rows // tile, own_rows // tile
    halo_start = (rows - SHORT) // tile
    row_spec = functools.partial(ordered, tiles=tiles, per_device=per_device)

    def halo_index(i, meta):
        return (0, jnp.maximum(lax.rem(i + (meta[PLACE] + 1) * per_device, tiles) - halo_start, 0), 0)

    return pl.pallas_call(
        functools.partial(settle_kernel, send_tiles, halo_start, tiles, per_device),
        grid_spec=pltpu.PrefetchScalarGridSpec(
            num_scalar_prefetch=1,
            grid=(tiles,),
            in_specs=[row_spec(tile, width), row_spec(tile, LANES), row_spec(tile, 2 * LANES), row_spec(tile, width)]
            + [row_spec(tile, head_width)] * 8
            + [pl.BlockSpec((2, tile, head_width), halo_index)] * 2
            + [whole(value.shape) for value in (*triples, left, *outputs)]
            + [at_columns((LANES, 3 * head_width), which) for which in (OWN, FAR)]
            + [at_rows((head_width, LANES), which) for which in (OWN, FAR)],
            out_specs=[
                row_spec(tile, width),
                sent(tile, width + LANES, send_tiles),
                kept(tile, width + LANES, send_tiles),
                held((LANES, 3 * head_width)),
                held((LANES, 3 * head_width)),
                held((LANES, width)),
                held((LANES, head_width)),
                held((LANES, head_width)),
            ],
        ),
        out_shape=[
            shaped((rows, width), F32),
            shaped((send_rows, width + LANES), BF16),
            shaped((own_rows, width + LANES), BF16),
            shaped((LANES, 3 * head_width), F32),
            shaped((LANES, 3 * head_width), F32),
            shaped((LANES, width), F32),
            shaped((LANES, head_width), F32),
            shaped((LANES, head_width), F32),
        ],
        compiler_params=params(),
        cost_estimate=BRIEF,
        name="settle",
    )(meta, normed, low, grad_lows, out, *pairs, *halos, *triples, left, *outputs, right, right, output_left,
      output_left)


def finish_kernel(
    parts, x_ref, dy_ref, gain1_ref, gain2_ref, output_right_ref, shrink_right_ref, *refs
):
    attention, feed = refs[:parts], refs[parts : 2 * parts]
    y_ref, dx_ref, norms_ref, output_right_grad_ref, shrink_right_grad_ref = refs[2 * parts :]
    width = x_ref.shape[1]

    def total(values, start, size):
        value = values[0][:, start : start + size].astype(F32)
        for other in values[1:]:
            value = value + other[:, start : start + size].astype(F32)
        return value

    out = total(feed, 0, width)
    first = total(attention, 0, width)
    second = total(feed, width, width)
    low_att = total(attention, width, LANES).astype(BF16)
    low_act = total(feed, 2 * width, LANES).astype(BF16)
    x = x_ref[...].astype(F32)
    dy = dy_ref[...]
    y_ref[...] = (
        x + out + dot_nn(low_att, output_right_ref[...]) + dot_nn(low_act, shrink_right_ref[...])
    ).astype(BF16)
    center = x - jnp.mean(x, axis=-1, keepdims=True)
    spread = jnp.mean(center * center, axis=-1, keepdims=True)
    inverse = lax.rsqrt(spread + EPS)
    unit = center * inverse
    scaled = first * gain1_ref[...] + second * gain2_ref[...]
    mean = jnp.mean(scaled, axis=-1, keepdims=True)
    inner = jnp.mean(scaled * unit, axis=-1, keepdims=True)
    dx_ref[...] = dy.astype(F32) + (scaled - mean - unit * inner) * inverse

    @pl.when(pl.program_id(0) == 0)
    def _():
        norms_ref[...] = jnp.zeros_like(norms_ref)
        output_right_grad_ref[...] = jnp.zeros_like(output_right_grad_ref)
        shrink_right_grad_ref[...] = jnp.zeros_like(shrink_right_grad_ref)

    norms_ref[0:1, :] += jnp.sum(first * unit, axis=0, keepdims=True)
    norms_ref[1:2, :] += jnp.sum(first, axis=0, keepdims=True)
    norms_ref[2:3, :] += jnp.sum(second * unit, axis=0, keepdims=True)
    norms_ref[3:4, :] += jnp.sum(second, axis=0, keepdims=True)
    output_right_grad_ref[...] += dot_tn(low_att, dy)
    shrink_right_grad_ref[...] += dot_tn(low_act, dy)


def finish(x, dy, gain1, gain2, output_right, shrink_right, attention, feed, tile):
    rows, width = x.shape
    parts = len(attention)
    return pl.pallas_call(
        functools.partial(finish_kernel, parts),
        grid=(rows // tile,),
        in_specs=[rows_of(tile, width)] * 2
        + [whole((1, width))] * 2
        + [whole(output_right.shape)] * 2
        + [rows_of(tile, width + LANES)] * parts
        + [rows_of(tile, 2 * width + LANES)] * parts,
        out_specs=[rows_of(tile, width)] * 2 + [held((8, width)), held((LANES, width)), held((LANES, width))],
        out_shape=[
            shaped((rows, width), BF16),
            shaped((rows, width), F32),
            shaped((8, width), F32),
            shaped((LANES, width), F32),
            shaped((LANES, width), F32),
        ],
        compiler_params=params(),
        cost_estimate=BRIEF,
        name="finish",
    )(x, dy, gain1, gain2, output_right, shrink_right, *attention, *feed)


SUM_ROWS = (2, 4, 16)


def sum_kernel(chunks, width, extra, part_ref, both_ref, out_ref, both_out_ref, *scratch):
    dp = lax.axis_index("dp")
    mp = lax.axis_index("mp")
    half, core = mp // 2, lax.rem(mp, 2)
    x, z = lax.rem(dp, 2), dp // 2
    x_peer = (dp + 1 - 2 * x, mp)
    y_peer = (dp, mp + 2 - 4 * half)
    core_peer = (dp, mp + 1 - 2 * core)
    z_places = [lax.rem(z + j, 4) for j in range(1, 4)]
    z_peers = [(place * 2 + x, mp) for place in z_places]
    barrier = pltpu.get_barrier_semaphore()
    for peer in [x_peer, y_peer, core_peer] + z_peers:
        pl.semaphore_signal(barrier, inc=1, device_id=peer, device_id_type=MESH)
    pl.semaphore_wait(barrier, 6)
    started = []

    def send(src, dst, sems, slot, peer):
        copy = pltpu.make_async_remote_copy(
            src_ref=src, dst_ref=dst, send_sem=sems.at[0, slot], recv_sem=sems.at[1, slot], device_id=peer,
            device_id_type=MESH,
        )
        copy.start()
        started.append(copy)
        return copy

    def added(first, *others):
        total = first.astype(F32)
        for other in others:
            total = total + other.astype(F32)
        return total.astype(BF16)

    both_got_ref, both_sum_ref, core_sems, local_sems = scratch[:4]
    refs = [scratch[4 + 7 * i : 4 + 7 * (i + 1)] for i in range(len(chunks))]
    both_copy = send(both_ref.at[1 - core], both_got_ref, core_sems, 0, core_peer)

    def run(index):
        y_first, start, size = chunks[index]
        got1, work1, got2, work2, got_z, full, sems = refs[index]
        shared = start is None
        if shared:
            both_copy.wait_recv()
            for place, at in ((0, half), (1, 1 - half)):
                both_sum_ref[place] = added(both_ref[core, at], both_got_ref[at])
            source = both_sum_ref
        else:
            source = part_ref.at[:, :, :, :, pl.ds(start, size)]
        if y_first:
            copy = send(source.at[1], got1, sems, 0, y_peer)
            yield
            copy.wait_recv()
            work1[...] = added(source[0], got1[...])
            copy = send(work1.at[1 - x], got2, sems, 1, x_peer)
            yield
            copy.wait_recv()
            work2[...] = added(work1[x], got2[...])
        else:
            copy = send(source.at[:, 1 - x], got1, sems, 0, x_peer)
            yield
            copy.wait_recv()
            work1[...] = added(source[:, x], got1[...])
            copy = send(work1.at[1], got2, sems, 1, y_peer)
            yield
            copy.wait_recv()
            work2[...] = added(work1[0], got2[...])
        copies = [
            send(work2.at[place], got_z.at[j], sems, 2 + j, peer)
            for j, (place, peer) in enumerate(zip(z_places, z_peers))
        ]
        yield
        for copy in copies:
            copy.wait_recv()
        full[0, x, z] = added(work2[z], got_z[0], got_z[1], got_z[2])
        mine = full.at[0, x, z]
        copies = [send(mine, mine, sems, 5 + j, peer) for j, peer in enumerate(z_peers)]
        yield
        for copy in copies:
            copy.wait_recv()
        if y_first:
            copy = send(full.at[0, x], full.at[0, x], sems, 8, x_peer)
            yield
            copy.wait_recv()
            copy = send(full.at[0], full.at[1], sems, 9, y_peer)
        else:
            copy = send(full.at[0, x], full.at[1, x], sems, 8, y_peer)
            yield
            copy.wait_recv()
            copy = send(full.at[:, x], full.at[:, x], sems, 9, x_peer)
        yield
        copy.wait_recv()
        target = both_out_ref if shared else out_ref.at[:, :, :, :, :, pl.ds(start, size)]
        last = []
        for place, at in ((0, half), (1, 1 - half)):
            local = pltpu.make_async_copy(full.at[place], target.at[core, at], local_sems.at[index, place])
            local.start()
            last.append(local)
            last.append(send(full.at[place], target.at[core, at], sems, 10 + place, core_peer))
        yield
        last[0].wait()
        last[1].wait_recv()
        last[2].wait()
        last[3].wait_recv()

    running = [run(i) for i in range(len(chunks))]
    while running:
        running = [step for step in running if next(step, "end") != "end"]
    for copy in started:
        copy.wait_send()


def sum_all(part, both):
    width, extra = part.shape[-1], both.shape[-1]
    third = width // 3
    chunks = [(True, 0, third), (False, third, third), (True, 2 * third, third), (False, None, extra)]
    per_chunk = []
    for y_first, _, size in chunks:
        one = (16, size)
        per_chunk += [
            pltpu.VMEM(((2, 4) if y_first else (2, 4)) + one, BF16),
            pltpu.VMEM((2, 4) + one, BF16),
            pltpu.VMEM((4,) + one, BF16),
            pltpu.VMEM((4,) + one, BF16),
            pltpu.VMEM((3,) + one, BF16),
            pltpu.VMEM((2, 2, 4) + one, BF16),
            pltpu.SemaphoreType.DMA((2, 12)),
        ]
    out, both_out = pl.pallas_call(
        functools.partial(sum_kernel, chunks, width, extra),
        out_shape=[shaped((2, 2) + SUM_ROWS + (width,), BF16), shaped((2, 2) + SUM_ROWS + (extra,), BF16)],
        in_specs=[pl.BlockSpec(memory_space=pltpu.VMEM)] * 2,
        out_specs=[pl.BlockSpec(memory_space=pl.ANY)] * 2,
        scratch_shapes=[
            pltpu.VMEM((2,) + SUM_ROWS + (extra,), BF16),
            pltpu.VMEM((2,) + SUM_ROWS + (extra,), BF16),
            pltpu.SemaphoreType.DMA((2, 1)),
            pltpu.SemaphoreType.DMA((len(chunks), 2)),
        ]
        + per_chunk,
        compiler_params=pltpu.CompilerParams(
            collective_id=2, has_side_effects=True, vmem_limit_bytes=VMEM_LIMIT
        ),
        cost_estimate=BRIEF,
        name="sum_all",
    )(part.reshape((2,) + SUM_ROWS + (width,)), both.reshape((2, 2) + SUM_ROWS + (extra,)))
    return out.reshape(2, 2, 128, width), both_out.reshape(2, 2, 128, extra)


def unpack_kernel(widths, part_ref, both_ref, triple_ref, output_ref, up_ref, down_ref, triple_left_ref,
                  up_left_ref, output_right_ref, down_right_ref, norm_ref):
    triple_width, head_width, hidden = widths
    start = triple_width
    triple_ref[...] = part_ref[0, 0, :, :triple_width].astype(F32)
    output_ref[...] = part_ref[0, 0, :, start : start + head_width].astype(F32).T
    start += head_width
    up_ref[...] = part_ref[0, 0, :, start : start + hidden].astype(F32)
    start += hidden
    down_ref[...] = part_ref[0, 0, :, start : start + hidden].astype(F32).T
    size = triple_left_ref.shape[0]
    triple_left_ref[...] = both_ref[0, 0, :, :size].astype(F32).T
    up_left_ref[...] = both_ref[0, 0, :, size : 2 * size].astype(F32).T
    output_right_ref[...] = both_ref[0, 0, :, 2 * size : 3 * size].astype(F32)
    down_right_ref[...] = both_ref[0, 0, :, 3 * size : 4 * size].astype(F32)
    norm_ref[0] = both_ref[0, 0, : norm_ref.shape[1], 4 * size :].astype(F32)


def unpack(part, both, width, triple_width, head_width, hidden):
    quarter = width // 4

    def tall(rows):
        return pl.BlockSpec((rows, LANES), lambda s: (s, 0))

    def wide(cols):
        return pl.BlockSpec((LANES, cols), lambda s: (0, s))

    def piece(cols):
        return pl.BlockSpec((1, 1, LANES, cols), lambda s: (lax.rem(s, 2), s // 2, 0, 0))

    return pl.pallas_call(
        functools.partial(unpack_kernel, (triple_width, head_width, hidden)),
        grid=(4,),
        in_specs=[piece(part.shape[-1]), piece(both.shape[-1])],
        out_specs=[
            wide(triple_width), tall(head_width), wide(hidden), tall(hidden), tall(quarter), tall(quarter),
            wide(quarter), wide(quarter), pl.BlockSpec((1, width // LANES, LANES), lambda s: (s, 0, 0)),
        ],
        out_shape=[
            shaped((LANES, 4 * triple_width), F32),
            shaped((4 * head_width, LANES), F32),
            shaped((LANES, 4 * hidden), F32),
            shaped((4 * hidden, LANES), F32),
            shaped((width, LANES), F32),
            shaped((width, LANES), F32),
            shaped((LANES, width), F32),
            shaped((LANES, width), F32),
            shaped((4, width // LANES, LANES), F32),
        ],
        compiler_params=params(),
        cost_estimate=BRIEF,
        name="unpack",
    )(part, both)


def shards(
    ranks,
    groups,
    block_input,
    sequence_lengths,
    first_gain,
    first_shift,
    second_gain,
    second_shift,
    triple_weight,
    triple_left,
    triple_right,
    output_weight,
    output_left,
    output_right,
    expand_weight,
    expand_left,
    expand_right,
    shrink_weight,
    shrink_left,
    shrink_right,
    cotangent,
):
    unit = ranks // 2
    own_rows, width = block_input.shape
    rows = own_rows * unit
    blocks = rows // SHORT
    tile = math.gcd(own_rows, 256)
    triple_width = triple_weight.shape[1]
    head_width = output_weight.shape[0]
    hidden = expand_weight.shape[1]
    mp = lax.axis_index("mp")
    half = mp // unit
    place = lax.rem(mp, unit)
    far = lax.rem(mp + unit, ranks)
    swap = [(m, (m + unit) % ranks) for m in range(ranks)]
    onward = [(m, m + unit) for m in range(unit)]
    back = [(m + unit, m) for m in range(unit)]

    tables = rotary_tables()
    dp = lax.axis_index("dp")
    lead = lax.rem(dp, 2)
    beside = [(d, d + 1 - 2 * (d % 2)) for d in range(groups)]
    continues = find_flags(sequence_lengths[0])
    conts = lax.dynamic_slice_in_dim(continues, half * blocks, blocks, 0)
    meta = jnp.concatenate([jnp.stack([mp, far, lead, place]).astype(jnp.int32), conts])
    gain1, shift1 = first_gain[None, :], first_shift[None, :]
    gain2, shift2 = second_gain[None, :], second_shift[None, :]

    x, dy = unit_gather(unit, block_input, cotangent)
    x_halo = lax.ppermute(x[rows - SHORT :], "mp", onward)

    def over_y(matrix):
        count = matrix.shape[0] // 2
        return lax.ppermute(lax.dynamic_slice_in_dim(matrix, lead * count, count, 0), "mp", swap)

    def over_x(piece):
        return lax.ppermute(piece, "dp", beside)

    (normed2, low2, grad_lows, out, grad2, low_act, grad_low2, expand_right_own, shrink_left_own, triple_far,
     output_far) = feed_first(
        unit, x, dy, gain2, shift2, expand_weight, expand_left, expand_right, shrink_weight, shrink_left, output_right,
        shrink_right, triple_weight, output_weight, tile,
    )
    expand_weight_late, shrink_weight_late, grad_lows = lax.optimization_barrier(
        (expand_weight, shrink_weight, grad_lows)
    )
    expand_piece = over_y(expand_weight_late)
    shrink_piece = over_y(shrink_weight_late)
    normed1, low1, q, k, v, g = project(
        meta, x_halo, x, dy, grad_lows, gain1, shift1, (triple_weight, triple_far), triple_left, triple_right,
        (output_weight, output_far), output_left, tables, tile,
    )
    count = 256
    att_far, gq_far, gk_far, gv_far, halo = attend(1, meta, q, k, v, g, tables, count)
    halo_own = lax.ppermute(halo, "mp", back)
    expand_piece, q = lax.optimization_barrier((expand_piece, q))
    expand_other = over_x(expand_piece)
    att_own, gq_own, gk_own, gv_own, halo = attend(0, meta, q, k, v, g, tables, count)
    halo_far = lax.ppermute(halo, "mp", back)
    shrink_piece, att_own = lax.optimization_barrier((shrink_piece, att_own))
    shrink_other = over_x(shrink_piece)
    (out, send1, keep1, triple_right_own, triple_right_far, triple_left_sum, output_left_sum_own,
     output_left_sum_far) = settle(
        meta, normed1, low1, grad_lows, out,
        (att_own, att_far, gq_own, gq_far, gk_own, gk_far, gv_own, gv_far), (halo_own, halo_far),
        (triple_weight, triple_far), triple_left, (output_weight, output_far), triple_right, output_left, own_rows, tile,
    )
    send2, keep2, expand_right_far, shrink_left_far, expand_left_sum = feed_second(
        meta, normed2, low2, dy, grad_lows, out, grad2, low_act, grad_low2, (expand_piece, expand_other), expand_left,
        expand_right, (shrink_piece, shrink_other), shrink_left, own_rows, tile,
    )

    def pass_on(sent_rows):
        got = []
        for j in range(1, unit):
            ring = [(m, m - m % unit + (m % unit + j) % unit) for m in range(ranks)]
            got.append(lax.ppermute(sent_rows[(j - 1) * own_rows : j * own_rows], "mp", ring))
        return got

    block_output, input_gradient, norms, output_right_sum, shrink_right_sum = finish(
        block_input, cotangent, gain1, gain2, output_right, shrink_right, [keep1] + pass_on(send1),
        [keep2] + pass_on(send2), math.gcd(own_rows, 128),
    )

    own_sums = (triple_right_own, output_left_sum_own, expand_right_own, shrink_left_own)
    far_sums = (triple_right_far, output_left_sum_far, expand_right_far, shrink_left_far)
    both_sums = (triple_left_sum, expand_left_sum, output_right_sum, shrink_right_sum)
    if ranks == 4 and groups == 8:
        part = jnp.stack(
            [jnp.concatenate([value.astype(BF16) for value in sums], axis=1) for sums in (own_sums, far_sums)]
        )
        quarters = [value.astype(BF16).reshape(LANES, 4, width // 4) for value in both_sums]
        norms = jnp.pad(
            norms[:4].astype(BF16).reshape(4, width // LANES, LANES), ((0, 0), (0, LANES - width // LANES), (0, 0))
        )
        both = jnp.concatenate([value.transpose(1, 0, 2) for value in quarters] + [norms], axis=2)
        both = both.reshape(2, 2, LANES, width + LANES).transpose(1, 0, 2, 3)
        part, both = sum_all(part, both)
        (triple_right_sum, output_left_sum, expand_right_sum, shrink_left_sum, triple_left_sum, expand_left_sum,
         output_right_sum, shrink_right_sum, norms) = unpack(
            part, both, width, triple_width, head_width, hidden
        )
        norms = norms.reshape(4, width)
    else:

        def spread(own, other):
            size = own.shape[1]
            wide = jnp.zeros((LANES, size * ranks), BF16)
            wide = lax.dynamic_update_slice_in_dim(wide, own.astype(BF16), mp * size, 1)
            return lax.dynamic_update_slice_in_dim(wide, other.astype(BF16), far * size, 1)

        sums = [spread(own, other) for own, other in zip(own_sums, far_sums)]
        sums += [value.astype(BF16) for value in both_sums]
        norms, *sums = lax.psum([norms] + sums, ("dp", "mp"))
        (triple_right_sum, output_left_sum, expand_right_sum, shrink_left_sum, triple_left_sum, expand_left_sum,
         output_right_sum, shrink_right_sum) = [value.astype(F32) for value in sums]
        output_left_sum, shrink_left_sum = output_left_sum.T, shrink_left_sum.T
        triple_left_sum, expand_left_sum = triple_left_sum.T, expand_left_sum.T
    return (
        block_output,
        input_gradient,
        norms[0],
        norms[1],
        norms[2],
        norms[3],
        triple_left_sum,
        triple_right_sum,
        output_left_sum,
        output_right_sum,
        expand_left_sum,
        expand_right_sum,
        shrink_left_sum,
        shrink_right_sum,
    )


def solution(mesh):
    placed = (
        P(("dp", "mp"), None),
        P("dp", None),
        P(),
        P(),
        P(),
        P(),
        P(None, "mp"),
        P(),
        P(),
        P("mp", None),
        P(),
        P(),
        P(None, "mp"),
        P(),
        P(),
        P("mp", None),
        P(),
        P(),
        P(("dp", "mp"), None),
    )
    return jax.shard_map(
        functools.partial(shards, mesh.shape["mp"], mesh.shape["dp"]),
        mesh=mesh,
        in_specs=placed,
        out_specs=(P(("dp", "mp"), None), P(("dp", "mp"), None)) + (P(),) * 12,
        check_vma=False,
    )
```

profile of v0, /device:TPU:1, one launch (start us, length us, event | category | flops | bytes accessed | tf_op | source)
XLA Modules:
  0.0 330.8 jit_solution(7045002141821687872)
XLA Ops:
  0.6 7.7 %unit_gather.1 = (bf16[1536,1024]{1,0:T(8,128)(2,1)}, bf16[1536,1024]{1,0:T(8,128)(2,1)}) custom-call(bf16[768,1024]{1,0:T(8,128)(2,1)} %x_ref.3, bf16[768,1024]{1,0:T(8,128)(2,1)} %dy_ref.1), custom_call_target="tpu_custom_call" | custom-call | flops 1 | bytes 1 | tf_op jit(solution)/shard_map/unit_gather/pallas_call | solution.py:158
  8.4 2.3 slice.23
  10.7 4.3 %collective-permute-start = (bf16[512,1024]{1,0:T(8,128)(2,1)}, bf16[512,1024]{1,0:T(8,128)(2,1)S(1)}, u32[]{:S(2)}, u32[]{:S(2)}) collective-permute-start(bf16[512,1024]{1,0:T(8,128)(2,1)} %slice.23), channel_id=1, source_target_pairs={{0,2},{1,3},{4,6},{5,7},{8,10},{9,11},{12,14},{13,15},{16,18},{17,... | collective-permute-start | bytes 3145736 | tf_op jit(solution)/shard_map/ppermute | solution.py:1150
  15.0 47.2 %feed_first.1 = (bf16[1536,1024]{1,0:T(8,128)(2,1)}, bf16[1536,128]{1,0:T(8,128)(2,1)}, bf16[1536,256]{1,0:T(8,128)(2,1)}, f32[1536,1024]{1,0:T(8,128)}, f32[153...) custom-call(bf16[1536,1024]{1,0:T(8,128)(2,1)} %get-tuple-element.79, ...), custom_call_target="tpu_custom_call" | custom-call | flops 1 | bytes 1 | tf_op jit(solution)/shard_map/feed_first/pallas_call | solution.py:307
  62.2 1.1 constant_dynamic-slice_fusion
  63.3 10.6 %collective-permute-start.2 = (bf16[512,1024]{1,0:T(8,128)(2,1)}, bf16[512,1024]{1,0:T(8,128)(2,1)S(1)}, u32[]{:S(2)}, u32[]{:S(2)}) collective-permute-start(bf16[512,1024]{1,0:T(8,128)(2,1)} %constant_dynamic-slice_fusion), channel_id=1, source_target_pairs={{0,2},{1,3},{2,0},{3,1},{4,6},{5,7},{6,4},{7,5},{8,10},{9,11},{10,... | collective-permute-start | bytes 3145736 | tf_op jit(solution)/shard_map/ppermute | solution.py:1154
  77.1 23.9 %project.1 = (bf16[1536,1024]{1,0:T(8,128)(2,1)}, bf16[1536,128]{1,0:T(8,128)(2,1)}, bf16[1536,512]{1,0:T(8,128)(2,1)}, bf16[2048,512]{1,0:T(8,128)(2,1)}, bf16[...) custom-call(s32[7]{0:T(128)} %concatenate.13.meta_ref, bf16[512,1024]{1,0:T(8,128)(2,1)} %copy-done.4, ...), custom_call_target="tpu_custom_call" | custom-call | flops 1 | bytes 1 | tf_op jit(solution)/shard_map/project/pallas_call | solution.py:548
  101.0 22.8 %attend.2 = (bf16[1536,256]{1,0:T(8,128)(2,1)}, bf16[1536,256]{1,0:T(8,128)(2,1)}, bf16[1536,256]{1,0:T(8,128)(2,1)}, bf16[1536,256]{1,0:T(8,128)(2,1)}, bf16[2,512,256]{2,1,0:T(8,128)(2,1)}) custom-call(s32[7]{0:T(128)} %concatenate.13.meta_ref, bf16[1536,512]{1,0:T(8,128)(2,1)} %get-tuple-element.91.q_ref, ...), custom_call_target="tpu_custom_call" | custom-call | flops 1 | bytes 1 | tf_op jit(solution)/shard_map/attend/pallas_call | solution.py:704
  123.9 1.3 collective-permute-start.7
  125.4 22.9 %attend.3 = (bf16[1536,256]{1,0:T(8,128)(2,1)}, bf16[1536,256]{1,0:T(8,128)(2,1)}, bf16[1536,256]{1,0:T(8,128)(2,1)}, bf16[1536,256]{1,0:T(8,128)(2,1)}, bf16[2,512,256]{2,1,0:T(8,128)(2,1)}) custom-call(s32[7]{0:T(128)} %concatenate.13.meta_ref, bf16[1536,512]{1,0:T(8,128)(2,1)} %get-tuple-element.91.q_ref, ...), custom_call_target="tpu_custom_call" | custom-call | flops 1 | bytes 1 | tf_op jit(solution)/shard_map/attend/pallas_call | solution.py:704
  148.3 1.3 collective-permute-start.3
  149.6 1.3 collective-permute-start.4
  150.9 10.9 %collective-permute-done.3.halo0_ref = bf16[2,512,256]{2,1,0:T(8,128)(2,1)S(1)} collective-permute-done((bf16[2,512,256]{2,1,0:T(8,128)(2,1)}, bf16[2,512,256]{2,1,0:T(8,128)(2,1)S(1)}, u32[]{:S(2)}, u32[]{:S(2)}) %collective-permute-start.3) | collective-permute-done | bytes 524320 | tf_op jit(solution)/shard_map/ppermute | solution.py:1175
  161.8 11.2 %collective-permute-done.4.halo1_ref = bf16[2,512,256]{2,1,0:T(8,128)(2,1)S(1)} collective-permute-done((bf16[2,512,256]{2,1,0:T(8,128)(2,1)S(1)}, bf16[2,512,256]{2,1,0:T(8,128)(2,1)S(1)}, u32[]{:S(2)}, u32[]{:S(2)}) %collective-permute-start.4) | collective-permute-done | bytes 524320 | tf_op jit(solution)/shard_map/ppermute | solution.py:1179
  173.8 21.4 %settle.1 = (f32[1536,1024]{1,0:T(8,128)}, bf16[768,1152]{1,0:T(8,128)(2,1)}, bf16[768,1152]{1,0:T(8,128)(2,1)}, f32[128,768]{1,0:T(8,128)}, f32[128,768]{1,0:T(...) custom-call(s32[7]{0:T(128)} %concatenate.13.meta_ref, ...), custom_call_target="tpu_custom_call" | custom-call | flops 1 | bytes 1 | tf_op jit(solution)/shard_map/settle/pallas_call | solution.py:786
  196.6 29.6 %feed_second.1 = (bf16[768,2176]{1,0:T(8,128)(2,1)}, bf16[768,2176]{1,0:T(8,128)(2,1)}, f32[128,1024]{1,0:T(8,128)}, f32[128,1024]{1,0:T(8,128)}, f32[128,1024]{1,0:T(8,128)}) custom-call(s32[7]{0:T(128)} %concatenate.13.meta_ref, bf16[1536,1024]{1,0:T(8,128)(2,1)} %get-tuple-element.108.normed_ref, bf16[1536,128]{1,0:T(8,128)(2,1)} %get-tuple-element.109.low_ref, ...), custom_call_target="tpu_custom_call" | custom-call | flops 1 | bytes 1 | tf_op jit(solution)/shard_map/feed_second/pallas_call | solution.py:438
  226.2 3.0 collective-permute-start.8
  231.7 1.3 pad_maximum_fusion.part_ref
  233.0 4.2 %collective-permute-done.5.refs_1_ = bf16[768,1152]{1,0:T(8,128)(2,1)S(1)} collective-permute-done((bf16[768,1152]{1,0:T(8,128)(2,1)S(1)}, bf16[768,1152]{1,0:T(8,128)(2,1)S(1)}, u32[]{:S(2)}, u32[]{:S(2)}) %collective-permute-start.5) | collective-permute-done | bytes 1769504 | tf_op jit(solution)/shard_map/ppermute | solution.py:1197
  239.4 10.7 %finish.1 = (bf16[768,1024]{1,0:T(8,128)(2,1)}, f32[768,1024]{1,0:T(8,128)}, f32[8,1024]{1,0:T(8,128)}, f32[128,1024]{1,0:T(8,128)}, f32[128,1024]{1,0:T(8,128)}) custom-call(bf16[768,1024]{1,0:T(8,128)(2,1)} %x_ref.3, bf16[768,1024]{1,0:T(8,128)(2,1)} %dy_ref.1, f32[1,1024]{1,0:T(1,128)} %bitcast.81, f32[1,1024]{1,0:T(1,128)} %bitcast.83, ...), custom_call_target="tpu_custom_call" | custom-call | flops 1 | bytes 1 | tf_op jit(solution)/shard_map/finish/pallas_call | solution.py:874
  253.2 1.1 copy.46
  254.3 69.3 %sum_all.1 = (bf16[2,2,2,4,16,3072]{5,4,3,2,1,0:T(8,128)(2,1)}, bf16[2,2,2,4,16,1152]{5,4,3,2,1,0:T(8,128)(2,1)}) custom-call(bf16[2,2,4,16,3072]{4,3,2,1,0:T(8,128)(2,1)} %pad_maximum_fusion.part_ref, bf16[2,2,2,4,16,1152]{5,4,3,2,1,0:T(8,128)(2,1)} %bitcast.69), custom_call_target="tpu_custom_call" | custom-call | flops 1 | bytes 1 | tf_op jit(solution)/shard_map/sum_all/pallas_call | solution.py:1024
  323.6 5.9 %unpack.1 = (f32[128,3072]{1,0:T(8,128)}, f32[1024,128]{1,0:T(8,128)}, f32[128,4096]{1,0:T(8,128)}, f32[4096,128]{1,0:T(8,128)}, f32[1024,128]{1,0:T(8,128)}, /*...) custom-call(bf16[2,2,128,3072]{3,2,1,0:T(8,128)(2,1)} %bitcast.70, ...), custom_call_target="tpu_custom_call" | custom-call | flops 1 | bytes 1 | tf_op jit(solution)/shard_map/unpack/pallas_call | solution.py:1075
  329.5 1.3 slice_bitcast_fusion
  (85 shorter events, 13.1 us)
Async XLA Ops:
  10.7 65.5 %collective-permute-start = (bf16[512,1024]{1,0:T(8,128)(2,1)}, bf16[512,1024]{1,0:T(8,128)(2,1)S(1)}, u32[]{:S(2)}, u32[]{:S(2)}) collective-permute-start(bf16[512,1024]{1,0:T(8,128)(2,1)} %slice.23), channel_id=1, source_target_pairs={{0,2},{1,3},{4,6},{5,7},{8,10},{9,11},{12,14},{13,15},{16,18},{17,... | collective-permute-start | bytes 3145736 | tf_op jit(solution)/shard_map/ppermute | solution.py:1150
  15.0 47.2 %copy-start = (bf16[1024,1024]{1,0:T(8,128)(2,1)S(1)}, bf16[1024,1024]{1,0:T(8,128)(2,1)}, u32[]{:S(2)}) copy-start(bf16[1024,1024]{1,0:T(8,128)(2,1)} %up_ref.1) | copy-start | bytes 6291460
  62.2 11.7 %copy-start.1 = (bf16[1024,1024]{1,0:T(8,128)(2,1)S(1)}, bf16[1024,1024]{1,0:T(8,128)(2,1)}, u32[]{:S(2)}) copy-start(bf16[1024,1024]{1,0:T(8,128)(2,1)} %down_ref.1) | copy-start | bytes 6291460
  63.3 11.6 %copy-start.22 = (s32[1,6]{1,0:T(1,128)S(1)}, s32[1,6]{1,0:T(1,128)}, u32[]{:S(2)}) copy-start(s32[1,6]{1,0:T(1,128)} %param.23) | copy-start | bytes 76
  63.3 37.7 %collective-permute-start.2 = (bf16[512,1024]{1,0:T(8,128)(2,1)}, bf16[512,1024]{1,0:T(8,128)(2,1)S(1)}, u32[]{:S(2)}, u32[]{:S(2)}) collective-permute-start(bf16[512,1024]{1,0:T(8,128)(2,1)} %constant_dynamic-slice_fusion), channel_id=1, source_target_pairs={{0,2},{1,3},{2,0},{3,1},{4,6},{5,7},{6,4},{7,5},{8,10},{9,11},{10,... | collective-permute-start | bytes 3145736 | tf_op jit(solution)/shard_map/ppermute | solution.py:1154
  74.0 49.8 %collective-permute-start.1 = (bf16[512,1024]{1,0:T(8,128)(2,1)S(1)}, bf16[512,1024]{1,0:T(8,128)(2,1)}, u32[]{:S(2)}, u32[]{:S(2)}) collective-permute-start(bf16[512,1024]{1,0:T(8,128)(2,1)S(1)} %constant_dynamic-slice_fusion.1), channel_id=1, source_target_pairs={{0,2},{1,3},{2,0},{3,1},{4,6},{5,7},{6,4},{7,5},{8,10},{9,11},{10,... | collective-permute-start | bytes 3145736 | tf_op jit(solution)/shard_map/ppermute | solution.py:1154
  101.0 24.2 %copy-start.5 = (bf16[512,1024]{1,0:T(8,128)(2,1)}, bf16[512,1024]{1,0:T(8,128)(2,1)S(1)}, u32[]{:S(2)}) copy-start(bf16[512,1024]{1,0:T(8,128)(2,1)S(1)} %collective-permute-done.2.up0_ref) | copy-start | bytes 3145732
  123.8 25.8 %copy-start.21 = (bf16[2,512,256]{2,1,0:T(8,128)(2,1)S(1)}, bf16[2,512,256]{2,1,0:T(8,128)(2,1)}, u32[]{:S(2)}) copy-start(bf16[2,512,256]{2,1,0:T(8,128)(2,1)} %get-tuple-element.105) | copy-start | bytes 1572868
  123.9 71.4 %collective-permute-start.7 = (bf16[512,1024]{1,0:T(8,128)(2,1)}, bf16[512,1024]{1,0:T(8,128)(2,1)S(1)}, u32[]{:S(2)}, u32[]{:S(2)}) collective-permute-start(bf16[512,1024]{1,0:T(8,128)(2,1)} %collective-permute-done.1.down0_ref), channel_id=1, source_target_pairs={{0,4},{4,0},{8,12},{12,8},{16,20},{20,16},{24,28},{28,24},{1,5},{5... | collective-permute-start | bytes 3145736 | tf_op jit(solution)/shard_map/ppermute | solution.py:1157
  125.1 70.1 %collective-permute-start.6 = (bf16[512,1024]{1,0:T(8,128)(2,1)S(1)}, bf16[512,1024]{1,0:T(8,128)(2,1)S(1)}, u32[]{:S(2)}, u32[]{:S(2)}) collective-permute-start(bf16[512,1024]{1,0:T(8,128)(2,1)S(1)} %collective-permute-done.2.up0_ref), channel_id=1, source_target_pairs={{0,4},{4,0},{8,12},{12,8},{16,20},{20,16},{24,28},{28,24},{1,5},{5... | collective-permute-start | bytes 3145736 | tf_op jit(solution)/shard_map/ppermute | solution.py:1157
  148.3 13.5 %collective-permute-start.3 = (bf16[2,512,256]{2,1,0:T(8,128)(2,1)}, bf16[2,512,256]{2,1,0:T(8,128)(2,1)S(1)}, u32[]{:S(2)}, u32[]{:S(2)}) collective-permute-start(bf16[2,512,256]{2,1,0:T(8,128)(2,1)} %get-tuple-element.104), channel_id=1, source_target_pairs={{2,0},{3,1},{6,4},{7,5},{10,8},{11,9},{14,12},{15,13},{18,16},{19,... | collective-permute-start | bytes 1572872 | tf_op jit(solution)/shard_map/ppermute | solution.py:1175
  149.6 23.4 %collective-permute-start.4 = (bf16[2,512,256]{2,1,0:T(8,128)(2,1)S(1)}, bf16[2,512,256]{2,1,0:T(8,128)(2,1)S(1)}, u32[]{:S(2)}, u32[]{:S(2)}) collective-permute-start(bf16[2,512,256]{2,1,0:T(8,128)(2,1)S(1)} %copy-done.21), channel_id=1, source_target_pairs={{2,0},{3,1},{6,4},{7,5},{10,8},{11,9},{14,12},{15,13},{18,16},{19,... | collective-permute-start | bytes 1572872 | tf_op jit(solution)/shard_map/ppermute | solution.py:1179
  161.8 11.2 %copy-start.8 = (bf16[2,512,256]{2,1,0:T(8,128)(2,1)}, bf16[2,512,256]{2,1,0:T(8,128)(2,1)S(1)}, u32[]{:S(2)}) copy-start(bf16[2,512,256]{2,1,0:T(8,128)(2,1)S(1)} %collective-permute-done.3.halo0_ref) | copy-start | bytes 1572868
  195.3 1.3 copy-start.7
  196.6 32.6 %copy-start.20 = (bf16[768,1152]{1,0:T(8,128)(2,1)S(1)}, bf16[768,1152]{1,0:T(8,128)(2,1)}, u32[]{:S(2)}) copy-start(bf16[768,1152]{1,0:T(8,128)(2,1)} %get-tuple-element.107) | copy-start | bytes 5308420
  196.6 32.7 %copy-start.11 = (f32[128,1024]{1,0:T(8,128)S(1)}, f32[128,1024]{1,0:T(8,128)}, u32[]{:S(2)}) copy-start(f32[128,1024]{1,0:T(8,128)} %get-tuple-element.122) | copy-start | bytes 1572868
  196.6 32.8 %copy-start.10 = (f32[128,1024]{1,0:T(8,128)S(1)}, f32[128,1024]{1,0:T(8,128)}, u32[]{:S(2)}) copy-start(f32[128,1024]{1,0:T(8,128)} %get-tuple-element.123) | copy-start | bytes 1572868
  226.1 3.3 copy-start.12
  226.1 3.3 copy-start.17
  226.2 3.3 %copy-start.19 = (f32[128,256]{1,0:T(8,128)S(1)}, f32[128,256]{1,0:T(8,128)}, u32[]{:S(2)}) copy-start(f32[128,256]{1,0:T(8,128)} %get-tuple-element.121) | copy-start | bytes 393220
  226.2 11.3 %collective-permute-start.8 = (bf16[768,2176]{1,0:T(8,128)(2,1)}, bf16[768,2176]{1,0:T(8,128)(2,1)S(1)}, u32[]{:S(2)}, u32[]{:S(2)}) collective-permute-start(bf16[768,2176]{1,0:T(8,128)(2,1)} %get-tuple-element.117), channel_id=1, source_target_pairs={{0,1},{1,0},{2,3},{3,2},{4,5},{5,4},{6,7},{7,6},{8,9},{9,8},{10,11... | collective-permute-start | bytes 10027016 | tf_op jit(solution)/shard_map/ppermute | solution.py:1197
  229.2 8.0 %collective-permute-start.5 = (bf16[768,1152]{1,0:T(8,128)(2,1)S(1)}, bf16[768,1152]{1,0:T(8,128)(2,1)S(1)}, u32[]{:S(2)}, u32[]{:S(2)}) collective-permute-start(bf16[768,1152]{1,0:T(8,128)(2,1)S(1)} %copy-done.20), channel_id=1, source_target_pairs={{0,1},{1,0},{2,3},{3,2},{4,5},{5,4},{6,7},{7,6},{8,9},{9,8},{10,11... | collective-permute-start | bytes 5308424 | tf_op jit(solution)/shard_map/ppermute | solution.py:1197
  237.2 1.2 copy-start.3
  237.5 1.9 copy-start.2
  (8 other events, 8.1 us)
where the time goes:
time: 332 us; the launch traced here: 331 us
  Pallas kernels  261 us (79%)
  waiting for transfers between devices  26.6 us (8%)
  starting transfers between devices  23.1 us (7%)
  local copies, waits for them, and re-layouts  14.3 us (4%)
  other arithmetic  4.18 us (1%)
    pallas_call x1, Pallas kernels, sum_all(): pl.pallas_call(functools.partial(sum_kernel, chunks, width, extra), out_s...  69.3 us
    pallas_call x1, Pallas kernels, feed_first(): pl.pallas_call(functools.partial(feed_first_kernel, unit, steps), grid=(s...  47.2 us
    pallas_call x2, Pallas kernels, attend(): pl.pallas_call(functools.partial(attend_kernel, blocks, count), grid_spec...  45.8 us
    pallas_call x1, Pallas kernels, feed_second(): pl.pallas_call(functools.partial(feed_second_kernel, tiles), grid_spec=pl...  29.6 us
    pallas_call x1, Pallas kernels, project(): pl.pallas_call(functools.partial(project_kernel, halo_tiles), grid_spec=p...  23.9 us
    pallas_call x1, Pallas kernels, settle(): pl.pallas_call(functools.partial(settle_kernel, send_tiles, halo_start, t...  21.4 us
    ppermute x2, starting transfers between devices, over_y(): lax.ppermute(lax.dynamic_slice_in_dim(matrix, lead * count, count, 0), 'm...  11.6 us
    ppermute x1, waiting for transfers between devices, shards(): halo_far = lax.ppermute(halo, 'mp', back)  11.2 us
  transfers between devices with their start and end apart: 9, of which 4 were waited for; matrix products, arithmetic and copies ran while one was open for 1% of the time, Pallas kernels for 42%

commit v1 on v0

--- a/solution.py
+++ b/solution.py
@@ -118,59 +118,6 @@
     return pltpu.CompilerParams(
         dimension_semantics=("arbitrary",) * semantics, vmem_limit_bytes=VMEM_LIMIT
     )
-
-
-def unit_gather_kernel(unit, x_ref, d_ref, xg_ref, dg_ref, local_sem, send_sem, recv_sem):
-    dp = lax.axis_index("dp")
-    mp = lax.axis_index("mp")
-    place = lax.rem(mp, unit)
-    base = mp - place
-    peers = [(dp, base + lax.rem(place + j, unit)) for j in range(1, unit)]
-    barrier = pltpu.get_barrier_semaphore()
-    for peer in peers:
-        pl.semaphore_signal(barrier, inc=1, device_id=peer, device_id_type=MESH)
-    pl.semaphore_wait(barrier, unit - 1)
-    rows = x_ref.shape[0]
-    span = pl.ds(pl.multiple_of(place * rows, rows), rows)
-    copies = []
-    for which, (src, dst) in enumerate(((x_ref, xg_ref), (d_ref, dg_ref))):
-        for j, peer in enumerate(peers):
-            copies.append(
-                pltpu.make_async_remote_copy(
-                    src_ref=src,
-                    dst_ref=dst.at[span],
-                    send_sem=send_sem.at[which, j],
-                    recv_sem=recv_sem.at[which, j],
-                    device_id=peer,
-                    device_id_type=MESH,
-                )
-            )
-        copies.append(pltpu.make_async_copy(src, dst.at[span], local_sem.at[which]))
-    for copy in copies:
-        copy.start()
-    for copy in copies:
-        copy.wait()
-
-
-def unit_gather(unit, x, d):
-    rows, width = x.shape
-    anywhere = pl.BlockSpec(memory_space=pl.ANY)
-    return pl.pallas_call(
-        functools.partial(unit_gather_kernel, unit),
-        out_shape=[shaped((rows * unit, width), x.dtype)] * 2,
-        in_specs=[pl.BlockSpec(memory_space=pltpu.VMEM)] * 2,
-        out_specs=[anywhere] * 2,
-        scratch_shapes=[
-            pltpu.SemaphoreType.DMA((2,)),
-            pltpu.SemaphoreType.DMA((2, unit - 1)),
-            pltpu.SemaphoreType.DMA((2, unit - 1)),
-        ],
-        compiler_params=pltpu.CompilerParams(
-            collective_id=1, has_side_effects=True, vmem_limit_bytes=VMEM_LIMIT
-        ),
-        cost_estimate=BRIEF,
-        name="unit_gather",
-    )(x, d)
 
 
 def gelu_parts(hidden):
@@ -227,23 +174,103 @@
     pl.semaphore_wait(barrier, len(peers))
 
 
+def place_in_unit(unit):
+    mp = lax.axis_index("mp")
+    return lax.rem(mp, unit), mp - lax.rem(mp, unit)
+
+
+def unit_peers(unit):
+    place, base = place_in_unit(unit)
+    return [(lax.axis_index("dp"), base + lax.rem(place + unit - s, unit)) for s in range(1, unit)]
+
+
+def halo_copies(unit, x_ref, halo_ref, y_sems, unit_sems):
+    own_rows = x_ref.shape[0]
+    chunk = math.gcd(own_rows, 128)
+    dp = lax.axis_index("dp")
+    found = []
+    for k in range(SHORT // chunk):
+        row = unit * own_rows - SHORT + k * chunk
+        holder, start = row // own_rows, row % own_rows
+        target = halo_ref.at[pl.ds(k * chunk, chunk)]
+        over_y = pltpu.make_async_remote_copy(
+            src_ref=x_ref.at[pl.ds(start, chunk)], dst_ref=target, send_sem=y_sems.at[0, k], recv_sem=y_sems.at[1, k],
+            device_id=(dp, unit + holder), device_id_type=MESH,
+        )
+        spread = [
+            pltpu.make_async_remote_copy(
+                src_ref=target, dst_ref=target, send_sem=unit_sems.at[0, k, s - 1], recv_sem=unit_sems.at[1, k, s - 1],
+                device_id=(dp, unit + (holder + s) % unit), device_id_type=MESH,
+            )
+            for s in range(1, unit)
+        ]
+        found.append((holder, over_y, spread))
+    return found
+
+
 def feed_first_kernel(
-    unit, steps, x_ref, dy_ref, gain_ref, shift_ref, up_ref, up_left_ref, up_right_ref, down_ref, down_left_ref,
-    output_right_ref, down_right_ref, triple_ref, output_ref, normed_ref, low_ref, grad_lows_ref, out_ref, grad_ref,
-    low_act_ref, grad_low_ref, up_right_grad_ref, down_left_grad_ref, triple_far_ref, output_far_ref, act_ref, gh_ref,
-    y_sems, x_sems,
+    unit, tile, x_ref, dy_ref, gain1_ref, shift1_ref, gain2_ref, shift2_ref, up_ref, up_left_ref, up_right_ref, down_ref,
+    down_left_ref, output_right_ref, down_right_ref, x_all_ref, dy_all_ref, triple_ref, output_ref, normed1_ref,
+    normed_ref, dy_full_ref, low_ref, grad_lows_ref, out_ref, grad_ref, low_act_ref, grad_low_ref, up_right_grad_ref,
+    down_left_grad_ref, triple_far_ref, output_far_ref, halo_ref, up_half_ref, down_half_ref, act_ref, gh_ref, xs_ref,
+    x_got_ref, dy_got_ref, y_sems, x_sems, unit_sems, halo_y_sems, halo_unit_sems, local_sems,
 ):
     step = pl.program_id(0)
+    own_rows = x_all_ref.shape[0]
+    per_device = own_rows // tile
+    steps = unit * per_device
     chunks = y_sems.shape[1]
+    place, base = place_in_unit(unit)
+    half = base // unit
+    peers = unit_peers(unit)
     over_y, over_x = courier(
         unit, ((triple_ref, triple_far_ref), (output_ref, output_far_ref)), chunks, y_sems, x_sems
     )
+    halo = halo_copies(unit, x_all_ref, halo_ref, halo_y_sems, halo_unit_sems)
+    rows_out = [
+        pltpu.make_async_remote_copy(
+            src_ref=src, dst_ref=dst.at[j], send_sem=unit_sems.at[0, which, j], recv_sem=unit_sems.at[1, which, j],
+            device_id=peer, device_id_type=MESH,
+        )
+        for j, peer in enumerate(peers)
+        for which, (src, dst) in enumerate(((x_all_ref, x_got_ref), (dy_all_ref, dy_got_ref)))
+    ]
+    lead = chip_neighbours(unit)[0]
+    kept_halves = [
+        pltpu.make_async_copy(
+            src.at[pl.ds(pl.multiple_of(lead * dst.shape[0], dst.shape[0]), dst.shape[0])], dst, local_sems.at[j]
+        )
+        for j, (src, dst) in enumerate(((up_ref, up_half_ref), (down_ref, down_half_ref)))
+    ]
 
     @pl.when(step == 0)
     def _():
-        meet(chip_neighbours(unit)[1:])
-        for copy in over_y:
+        meet([*chip_neighbours(unit)[1:], *peers])
+        for copy in rows_out + over_y + kept_halves:
             copy.start()
+        xs_ref[...] = x_ref[...]
+        dy_full_ref[...] = dy_ref[...]
+
+    for holder, copy, _ in halo:
+        pl.when((step == 0) & (half == 0) & (place == holder))(copy.start)
+
+    @pl.when((step > 0) & (step < per_device))
+    def _():
+        xs_ref[...] = x_ref[...]
+        dy_full_ref[...] = dy_ref[...]
+
+    for slot in range(unit - 1):
+
+        @pl.when(step == per_device * (slot + 1))
+        def _():
+            for which in range(2):
+                rows_out[2 * slot + which].wait_recv()
+
+        @pl.when((step >= per_device * (slot + 1)) & (step < per_device * (slot + 2)))
+        def _():
+            span = pl.ds(pl.multiple_of((step - per_device * (slot + 1)) * tile, tile), tile)
+            xs_ref[...] = x_got_ref[slot, span]
+            dy_full_ref[...] = dy_got_ref[slot, span]
 
     for k in range(chunks):
 
@@ -253,9 +280,14 @@
                 over_y[j].wait_recv()
                 over_x[j].start()
 
-    normed = normalize(x_ref[...].astype(F32), gain_ref[...], shift_ref[...]).astype(BF16)
+    x = xs_ref[...].astype(F32)
+    center = x - jnp.mean(x, axis=-1, keepdims=True)
+    spread = jnp.mean(center * center, axis=-1, keepdims=True)
+    scaled = center * lax.rsqrt(spread + EPS)
+    normed1_ref[...] = (scaled * gain1_ref[...] + shift1_ref[...]).astype(BF16)
+    normed = (scaled * gain2_ref[...] + shift2_ref[...]).astype(BF16)
     normed_ref[...] = normed
-    dy = dy_ref[...]
+    dy = dy_full_ref[...]
     low = dot_nn(normed, up_left_ref[...]).astype(BF16)
     low_ref[...] = low
     rights = jnp.concatenate([output_right_ref[...], down_right_ref[...]], axis=0)
@@ -270,7 +302,7 @@
     low_act_ref[...] = dot_nn(act, down_left_ref[...])
     grad_low_ref[...] = dot_nt(gh, up_right_ref[...])
 
-    @pl.when(pl.program_id(0) == 0)
+    @pl.when(step == 0)
     def _():
         up_right_grad_ref[...] = jnp.zeros_like(up_right_grad_ref)
         down_left_grad_ref[...] = jnp.zeros_like(down_left_grad_ref)
@@ -278,11 +310,40 @@
     up_right_grad_ref[...] += dot_tn(low, gh)
     down_left_grad_ref[...] += dot_tn(grad_low, act)
 
+    @pl.when((step == 0) & (half == 0))
+    def _():
+        fills = [
+            pltpu.make_async_copy(xs_ref, halo_ref.at[pl.ds(k * tile, tile)], local_sems.at[2 + k])
+            for k in range(SHORT // tile)
+        ]
+        for copy in fills:
+            copy.start()
+        for copy in fills:
+            copy.wait()
+
     @pl.when(step == steps - 1)
     def _():
-        for copy in over_y:
+        for holder, copy, spread_copies in halo:
+
+            @pl.when((half == 1) & (place == holder))
+            def _():
+                copy.wait_recv()
+                for other in spread_copies:
+                    other.start()
+
+        for holder, copy, spread_copies in halo:
+            pl.when((half == 0) & (place == holder))(copy.wait_send)
+
+            @pl.when((half == 1) & (place == holder))
+            def _():
+                for other in spread_copies:
+                    other.wait_send()
+
+            for s in range(1, unit):
+                pl.when((half == 1) & (place == (holder + s) % unit))(spread_copies[s - 1].wait_recv)
+        for copy in rows_out + over_y:
             copy.wait_send()
-        for copy in over_x:
+        for copy in over_x + kept_halves:
             copy.wait()
 
 
@@ -297,21 +358,29 @@
 OWN, FAR, LEAD, PLACE, CONT = 0, 1, 2, 3, 4
 
 
-def feed_first(unit, x, dy, gain, shift, up, up_left, up_right, down, down_left, output_right, down_right, triple,
-               output, tile):
-    rows, width = x.shape
+def feed_first(unit, x, dy, norms, up, up_left, up_right, down, down_left, output_right, down_right, triple, output,
+               tile):
+    own_rows, width = x.shape
+    rows = own_rows * unit
     hidden = up.shape[1]
-    steps = rows // tile
+    steps, per_device = rows // tile, own_rows // tile
     chunks = math.gcd(4, output.shape[0] // 32)
+    halo_chunks = SHORT // math.gcd(own_rows, 128)
     anywhere = pl.BlockSpec(memory_space=pl.ANY)
+    here = pl.BlockSpec((tile, width), lambda i: (jnp.minimum(i, per_device - 1), 0))
+
+    def turned(size):
+        def index(i):
+            return (lax.rem(i + place_in_unit(unit)[0] * per_device, steps), 0)
+
+        return pl.BlockSpec((tile, size), index)
+
     return pl.pallas_call(
-        functools.partial(feed_first_kernel, unit, steps),
+        functools.partial(feed_first_kernel, unit, tile),
         grid=(steps,),
-        in_specs=[
-            rows_of(tile, width),
-            rows_of(tile, width),
-            whole((1, width)),
-            whole((1, width)),
+        in_specs=[here, here]
+        + [whole((1, width))] * 4
+        + [
             whole(up.shape),
             whole(up_left.shape),
             pl.BlockSpec((LANES, hidden), lambda i: (0, lax.axis_index("mp")), pipeline_mode=pl.Buffered(1)),
@@ -319,29 +388,38 @@
             pl.BlockSpec((hidden, LANES), lambda i: (lax.axis_index("mp"), 0), pipeline_mode=pl.Buffered(1)),
             whole(output_right.shape),
             whole(down_right.shape),
-            anywhere,
-            anywhere,
-        ],
+        ]
+        + [anywhere] * 4,
         out_specs=[
-            rows_of(tile, width),
-            rows_of(tile, LANES),
-            rows_of(tile, 2 * LANES),
-            rows_of(tile, width),
-            rows_of(tile, width),
-            rows_of(tile, LANES),
-            rows_of(tile, LANES),
+            turned(width),
+            turned(width),
+            turned(width),
+            turned(LANES),
+            turned(2 * LANES),
+            turned(width),
+            turned(width),
+            turned(LANES),
+            turned(LANES),
             held((LANES, hidden)),
             held((LANES, hidden)),
-            anywhere,
-            anywhere,
-        ],
+        ]
+        + [anywhere] * 5,
         scratch_shapes=[
             pltpu.VMEM((tile, hidden), BF16),
             pltpu.VMEM((tile, hidden), BF16),
+            pltpu.VMEM((tile, width), BF16),
+            pltpu.VMEM((unit - 1, own_rows, width), BF16),
+            pltpu.VMEM((unit - 1, own_rows, width), BF16),
             pltpu.SemaphoreType.DMA((2, chunks, 2)),
             pltpu.SemaphoreType.DMA((2, chunks, 2)),
+            pltpu.SemaphoreType.DMA((2, 2, unit - 1)),
+            pltpu.SemaphoreType.DMA((2, halo_chunks)),
+            pltpu.SemaphoreType.DMA((2, halo_chunks, unit - 1)),
+            pltpu.SemaphoreType.DMA((2 + SHORT // tile,)),
         ],
         out_shape=[
+            shaped((rows, width), BF16),
+            shaped((rows, width), BF16),
             shaped((rows, width), BF16),
             shaped((rows, LANES), BF16),
             shaped((rows, 2 * LANES), BF16),
@@ -353,13 +431,16 @@
             shaped((LANES, hidden), F32),
             shaped(triple.shape, BF16),
             shaped(output.shape, BF16),
+            shaped((SHORT, width), BF16),
+            shaped((up.shape[0] // 2, up.shape[1]), BF16),
+            shaped((down.shape[0] // 2, down.shape[1]), BF16),
         ],
         compiler_params=pltpu.CompilerParams(
             dimension_semantics=("arbitrary",), vmem_limit_bytes=VMEM_LIMIT, collective_id=3, has_side_effects=True
         ),
         cost_estimate=BRIEF,
         name="feed_first",
-    )(x, dy, gain, shift, up, up_left, up_right, down, down_left, output_right, down_right, triple, output)
+    )(x, dy, *norms, up, up_left, up_right, down, down_left, output_right, down_right, x, dy, triple, output)
 
 
 def join_halves(step, lead, pieces, whole_ref):
@@ -372,13 +453,38 @@
 
 
 def feed_second_kernel(
-    send_tiles, meta_ref, normed_ref, low_ref, dy_ref, grad_lows_ref, out_in_ref, grad_in_ref, low_act_in_ref,
-    grad_low_in_ref, up0_ref, up1_ref, up_left_ref, up_right_ref, down0_ref, down1_ref, down_left_ref, send_ref,
-    keep_ref, up_right_grad_ref, down_left_grad_ref, up_left_grad_ref, act_ref, gh_ref, up_ref, down_ref,
+    unit, tile, normed_ref, low_ref, dy_ref, grad_lows_ref, out_in_ref, grad_in_ref, low_act_in_ref, grad_low_in_ref,
+    x_ref, keep_ref, got1_ref, gain1_ref, gain2_ref, output_right_ref, down_right_ref, up0_ref, up1_ref, up_left_ref,
+    up_right_ref, down0_ref, down1_ref, down_left_ref, y_ref, dx_ref, norms_ref, output_right_grad_ref,
+    down_right_grad_ref, up_right_grad_ref, down_left_grad_ref, up_left_grad_ref, act_ref, gh_ref, up_ref, down_ref,
+    send_ref, got_ref, sems,
 ):
     step = pl.program_id(0)
-    join_halves(step, meta_ref[LEAD], (up0_ref, up1_ref), up_ref)
-    join_halves(step, meta_ref[LEAD], (down0_ref, down1_ref), down_ref)
+    own_rows = got_ref.shape[1]
+    per_device = own_rows // tile
+    send_tiles = (unit - 1) * per_device
+    lead = chip_neighbours(unit)[0]
+    peers = unit_peers(unit)
+    copies = [
+        [
+            pltpu.make_async_remote_copy(
+                src_ref=send_ref.at[s, pl.ds(t * tile, tile)], dst_ref=got_ref.at[s, pl.ds(t * tile, tile)],
+                send_sem=sems.at[0, s, t], recv_sem=sems.at[1, s, t], device_id=peer, device_id_type=MESH,
+            )
+            for t in range(per_device)
+        ]
+        for s, peer in enumerate(peers)
+    ]
+
+    @pl.when(step == 0)
+    def _():
+        meet(peers)
+        for ref in (norms_ref, output_right_grad_ref, down_right_grad_ref, up_right_grad_ref, down_left_grad_ref,
+                    up_left_grad_ref):
+            ref[...] = jnp.zeros_like(ref)
+
+    join_halves(step, lead, (up0_ref, up1_ref), up_ref)
+    join_halves(step, lead, (down0_ref, down1_ref), down_ref)
     normed = normed_ref[...]
     low = low_ref[...]
     dy = dy_ref[...]
@@ -387,118 +493,171 @@
     act = act_ref[...]
     gh = gh_ref[...]
     grad_low_up = (grad_low_in_ref[...] + dot_nt(gh, up_right_ref[...])).astype(BF16)
-    out = (out_in_ref[...] + dot_nn(act, down_ref[...])).astype(BF16)
-    low_act = (low_act_in_ref[...] + dot_nn(act, down_left_ref[...])).astype(BF16)
-    grad = (
-        grad_in_ref[...] + dot_nt(gh, up_ref[...]) + dot_nt(grad_low_up, up_left_ref[...])
-    ).astype(BF16)
-    width = out.shape[1]
-
-    def put(ref):
-        ref[:, :width] = out
-        ref[:, width : 2 * width] = grad
-        ref[:, 2 * width :] = low_act
-
-    pl.when(step < send_tiles)(lambda: put(send_ref))
-    pl.when(step >= send_tiles)(lambda: put(keep_ref))
-
-    @pl.when(step == 0)
-    def _():
-        up_right_grad_ref[...] = jnp.zeros_like(up_right_grad_ref)
-        down_left_grad_ref[...] = jnp.zeros_like(down_left_grad_ref)
-        up_left_grad_ref[...] = jnp.zeros_like(up_left_grad_ref)
+    width = dy.shape[1]
+
+    def results():
+        out = out_in_ref[...] + dot_nn(act, down_ref[...])
+        grad = grad_in_ref[...] + dot_nt(gh, up_ref[...]) + dot_nt(grad_low_up, up_left_ref[...])
+        low_act = low_act_in_ref[...] + dot_nn(act, down_left_ref[...])
+        return out, grad, low_act
 
     up_right_grad_ref[...] += dot_tn(low, gh)
     down_left_grad_ref[...] += dot_tn(grad_low, act)
     up_left_grad_ref[...] += dot_tn(grad_low_up, normed)
 
-
-def ordered(tile, width, tiles, per_device):
-    return pl.BlockSpec(
-        (tile, width), lambda i, meta: (lax.rem(i + (meta[PLACE] + 1) * per_device, tiles), 0)
-    )
-
-
-def sent(tile, width, tiles):
-    return pl.BlockSpec((tile, width), lambda i, meta: (jnp.minimum(i, tiles - 1), 0))
-
-
-def kept(tile, width, tiles):
-    return pl.BlockSpec((tile, width), lambda i, meta: (jnp.maximum(i - tiles, 0), 0))
-
-
-def feed_second(meta, normed, low, dy, grad_lows, out, grad, low_act, grad_low, ups, up_left, up_right, downs,
-                down_left, own_rows, tile):
+    @pl.when(step < send_tiles)
+    def _():
+        out, grad, low_act = results()
+        slot = step // per_device
+        span = pl.ds(pl.multiple_of(lax.rem(step, per_device) * tile, tile), tile)
+        send_ref[slot, span, :width] = out.astype(BF16)
+        send_ref[slot, span, width : 2 * width] = grad.astype(BF16)
+        send_ref[slot, span, 2 * width :] = low_act.astype(BF16)
+
+    for s in range(unit - 1):
+        for t in range(per_device):
+            pl.when(step == s * per_device + t)(copies[s][t].start)
+            pl.when(step == send_tiles + t)(copies[s][t].wait_recv)
+
+    @pl.when(step >= send_tiles)
+    def _():
+        out, second, low_act = results()
+        span = pl.ds(pl.multiple_of((step - send_tiles) * tile, tile), tile)
+        first = keep_ref[:, :width].astype(F32)
+        low_att = keep_ref[:, width:].astype(F32)
+        for s in range(unit - 1):
+            first = first + got1_ref[s, :, :width].astype(F32)
+            low_att = low_att + got1_ref[s, :, width:].astype(F32)
+            out = out + got_ref[s, span, :width].astype(F32)
+            second = second + got_ref[s, span, width : 2 * width].astype(F32)
+            low_act = low_act + got_ref[s, span, 2 * width :].astype(F32)
+        low_att, low_act = low_att.astype(BF16), low_act.astype(BF16)
+        x = x_ref[...].astype(F32)
+        y_ref[...] = (
+            x + out + dot_nn(low_att, output_right_ref[...]) + dot_nn(low_act, down_right_ref[...])
+        ).astype(BF16)
+        center = x - jnp.mean(x, axis=-1, keepdims=True)
+        spread = jnp.mean(center * center, axis=-1, keepdims=True)
+        inverse = lax.rsqrt(spread + EPS)
+        scaled = center * inverse
+        total = first * gain1_ref[...] + second * gain2_ref[...]
+        mean = jnp.mean(total, axis=-1, keepdims=True)
+        inner = jnp.mean(total * scaled, axis=-1, keepdims=True)
+        dx_ref[...] = dy.astype(F32) + (total - mean - scaled * inner) * inverse
+        norms_ref[0:1, :] += jnp.sum(first * scaled, axis=0, keepdims=True)
+        norms_ref[1:2, :] += jnp.sum(first, axis=0, keepdims=True)
+        norms_ref[2:3, :] += jnp.sum(second * scaled, axis=0, keepdims=True)
+        norms_ref[3:4, :] += jnp.sum(second, axis=0, keepdims=True)
+        output_right_grad_ref[...] += dot_tn(low_att, dy)
+        down_right_grad_ref[...] += dot_tn(low_act, dy)
+
+    @pl.when(step == unit * per_device - 1)
+    def _():
+        for group in copies:
+            for copy in group:
+                copy.wait_send()
+
+
+def feed_second(unit, normed, low, dy, grad_lows, out, grad, low_act, grad_low, x, keep, got, gains, output_right,
+                down_right, ups, up_left, up_right, downs, down_left, tile):
     rows, width = normed.shape
+    own_rows = rows // unit
     hidden = ups[0].shape[1]
-    send_rows = rows - own_rows
-    tiles = send_rows // tile
-    row_spec = functools.partial(ordered, tiles=rows // tile, per_device=own_rows // tile)
+    steps, per_device = rows // tile, own_rows // tile
+    send_tiles = steps - per_device
     wide = 2 * width + LANES
+
+    def turned(size):
+        def index(i):
+            place, slot = place_in_unit(unit)[0], i // per_device + 1
+            return (lax.rem(place + unit - slot, unit) * per_device + lax.rem(i, per_device), 0)
+
+        return pl.BlockSpec((tile, size), index)
+
+    def late(size):
+        return pl.BlockSpec((tile, size), lambda i: (jnp.maximum(i - send_tiles, 0), 0))
+
+    def far():
+        return lax.rem(lax.axis_index("mp") + unit, 2 * unit)
+
     return pl.pallas_call(
-        functools.partial(feed_second_kernel, tiles),
-        grid_spec=pltpu.PrefetchScalarGridSpec(
-            num_scalar_prefetch=1,
-            grid=(rows // tile,),
-            in_specs=[
-                row_spec(tile, width),
-                row_spec(tile, LANES),
-                row_spec(tile, width),
-                row_spec(tile, 2 * LANES),
-                row_spec(tile, width),
-                row_spec(tile, width),
-                row_spec(tile, LANES),
-                row_spec(tile, LANES),
-                whole(ups[0].shape),
-                whole(ups[1].shape),
-                whole(up_left.shape),
-                at_columns((LANES, hidden), FAR),
-                whole(downs[0].shape),
-                whole(downs[1].shape),
-                at_rows((hidden, LANES), FAR),
-            ],
-            out_specs=[
-                sent(tile, wide, tiles),
-                kept(tile, wide, tiles),
-                held((LANES, hidden)),
-                held((LANES, hidden)),
-                held((LANES, width)),
-            ],
-            scratch_shapes=[
-                pltpu.VMEM((tile, hidden), BF16),
-                pltpu.VMEM((tile, hidden), BF16),
-                pltpu.VMEM((width, hidden), BF16),
-                pltpu.VMEM((hidden, width), BF16),
-            ],
-        ),
+        functools.partial(feed_second_kernel, unit, tile),
+        grid=(steps,),
+        in_specs=[
+            turned(width),
+            turned(LANES),
+            turned(width),
+            turned(2 * LANES),
+            turned(width),
+            turned(width),
+            turned(LANES),
+            turned(LANES),
+            late(width),
+            late(width + LANES),
+            pl.BlockSpec((unit - 1, tile, width + LANES), lambda i: (0, jnp.maximum(i - send_tiles, 0), 0)),
+            whole((1, width)),
+            whole((1, width)),
+            whole(output_right.shape),
+            whole(down_right.shape),
+            whole(ups[0].shape),
+            whole(ups[1].shape),
+            whole(up_left.shape),
+            pl.BlockSpec((LANES, hidden), lambda i: (0, far()), pipeline_mode=pl.Buffered(1)),
+            whole(downs[0].shape),
+            whole(downs[1].shape),
+            pl.BlockSpec((hidden, LANES), lambda i: (far(), 0), pipeline_mode=pl.Buffered(1)),
+        ],
+        out_specs=[
+            late(width),
+            late(width),
+            held((8, width)),
+            held((LANES, width)),
+            held((LANES, width)),
+            held((LANES, hidden)),
+            held((LANES, hidden)),
+            held((LANES, width)),
+        ],
+        scratch_shapes=[
+            pltpu.VMEM((tile, hidden), BF16),
+            pltpu.VMEM((tile, hidden), BF16),
+            pltpu.VMEM((width, hidden), BF16),
+            pltpu.VMEM((hidden, width), BF16),
+            pltpu.VMEM((unit - 1, own_rows, wide), BF16),
+            pltpu.VMEM((unit - 1, own_rows, wide), BF16),
+            pltpu.SemaphoreType.DMA((2, unit - 1, per_device)),
+        ],
         out_shape=[
-            shaped((send_rows, wide), BF16),
-            shaped((own_rows, wide), BF16),
+            shaped((own_rows, width), BF16),
+            shaped((own_rows, width), F32),
+            shaped((8, width), F32),
+            shaped((LANES, width), F32),
+            shaped((LANES, width), F32),
             shaped((LANES, hidden), F32),
             shaped((LANES, hidden), F32),
             shaped((LANES, width), F32),
         ],
-        compiler_params=params(),
+        compiler_params=pltpu.CompilerParams(
+            dimension_semantics=("arbitrary",), vmem_limit_bytes=VMEM_LIMIT, collective_id=4, has_side_effects=True
+        ),
         cost_estimate=BRIEF,
         name="feed_second",
-    )(meta, normed, low, dy, grad_lows, out, grad, low_act, grad_low, *ups, up_left, up_right, *downs, down_left)
+    )(normed, low, dy, grad_lows, out, grad, low_act, grad_low, x, keep, got, *gains, output_right, down_right, *ups,
+      up_left, up_right, *downs, down_left)
 
 
 def project_kernel(
-    halo_tiles, meta_ref, x_halo_ref, x_ref, dy_ref, grad_lows_ref, gain_ref, shift_ref, triple0_ref, triple1_ref,
+    main_tiles, meta_ref, x_halo_ref, normed_ref, dy_ref, grad_lows_ref, gain_ref, shift_ref, triple0_ref, triple1_ref,
     left_ref, right0_ref, right1_ref, output0_ref, output1_ref, output_left0_ref, output_left1_ref, cos_ref,
-    minus_ref, plus_ref, normed_ref, low_ref, q_ref, k_ref, v_ref, g_ref,
+    minus_ref, plus_ref, low_ref, q_ref, k_ref, v_ref, g_ref,
 ):
     step = pl.program_id(0)
     tables = (cos_ref[...], minus_ref[...], plus_ref[...])
     head_width = output0_ref.shape[0]
     first = low_lanes()
 
-    def rows(x, full):
-        normed = normalize(x.astype(F32), gain_ref[...], shift_ref[...]).astype(BF16)
+    def rows(normed, full):
         low = dot_nn(normed, left_ref[...]).astype(BF16)
         if full:
-            normed_ref[...] = normed
             low_ref[...] = low
         for shard, (triple, right) in enumerate(((triple0_ref, right0_ref), (triple1_ref, right1_ref))):
             mixed = dot_nn(normed, triple[...]) + dot_nn(low, right[...])
@@ -514,44 +673,51 @@
                     query = rotate(jnp.where(first, one, two), *tables).astype(BF16)
                     q_ref[:, cols] = query * HEAD_DIM**-0.5
 
-    @pl.when(step < halo_tiles)
-    def _():
-        rows(x_halo_ref[...], False)
-
-    @pl.when(step >= halo_tiles)
-    def _():
-        rows(x_ref[...], True)
+    @pl.when(step < main_tiles)
+    def _():
+        rows(normed_ref[...], True)
         dy = dy_ref[...]
         grad_low = grad_lows_ref[:, :LANES]
         outputs = jnp.concatenate([output0_ref[...], output1_ref[...]], axis=0)
         lefts = jnp.concatenate([output_left0_ref[...], output_left1_ref[...]], axis=0)
         g_ref[...] = (dot_nt(dy, outputs) + dot_nt(grad_low, lefts)).astype(BF16)
 
-
-def project(meta, x_halo, x, dy, grad_lows, gain, shift, triples, left, right, outputs, output_left, tables, tile):
+    @pl.when(step >= main_tiles)
+    def _():
+        rows(normalize(x_halo_ref[...].astype(F32), gain_ref[...], shift_ref[...]).astype(BF16), False)
+
+
+def project(meta, x_halo, normed, dy, grad_lows, gain, shift, triples, left, right, outputs, output_left, tables, tile):
     rows, width = dy.shape
     head_width = outputs[0].shape[0]
     triple_width = triples[0].shape[1]
     per_block = SHORT // tile
-    halo_tiles = SHORT // tile
+    main_tiles, halo_tiles = rows // tile, SHORT // tile
 
     def table_index(i, meta):
-        j = jnp.maximum(i - halo_tiles, 0)
-        block = meta[CONT + j // per_block] * per_block + lax.rem(j, per_block)
-        return (jnp.where(i < halo_tiles, i, block), 0)
+        block = meta[CONT + jnp.minimum(i, main_tiles - 1) // per_block] * per_block + lax.rem(i, per_block)
+        return (jnp.where(i < main_tiles, block, i - main_tiles), 0)
 
     table = pl.BlockSpec((tile, LANES), table_index)
 
     def main(size):
-        return pl.BlockSpec((tile, size), lambda i, meta: (jnp.maximum(i - halo_tiles, 0), 0))
+        return pl.BlockSpec((tile, size), lambda i, meta: (jnp.minimum(i, main_tiles - 1), 0))
+
+    def late(size):
+        return pl.BlockSpec((tile, size), lambda i, meta: (jnp.maximum(i - main_tiles, 0), 0))
+
+    def all_rows(size):
+        return pl.BlockSpec(
+            (tile, size), lambda i, meta: (jnp.where(i < main_tiles, i + halo_tiles, i - main_tiles), 0)
+        )
 
     return pl.pallas_call(
-        functools.partial(project_kernel, halo_tiles),
+        functools.partial(project_kernel, main_tiles),
         grid_spec=pltpu.PrefetchScalarGridSpec(
             num_scalar_prefetch=1,
-            grid=(halo_tiles + rows // tile,),
+            grid=(main_tiles + halo_tiles,),
             in_specs=[
-                pl.BlockSpec((tile, width), lambda i, meta: (jnp.minimum(i, halo_tiles - 1), 0)),
+                late(width),
                 main(width),
                 main(width),
                 main(2 * LANES),
@@ -571,16 +737,14 @@
                 table,
             ],
             out_specs=[
-                main(width),
                 main(LANES),
                 main(2 * head_width),
-                rows_of(tile, 2 * head_width),
-                rows_of(tile, 2 * head_width),
+                all_rows(2 * head_width),
+                all_rows(2 * head_width),
                 main(2 * head_width),
             ],
         ),
         out_shape=[
-            shaped((rows, width), BF16),
             shaped((rows, LANES), BF16),
             shaped((rows, 2 * head_width), BF16),
             shaped((SHORT + rows, 2 * head_width), BF16),
@@ -590,8 +754,8 @@
         compiler_params=params(),
         cost_estimate=BRIEF,
         name="project",
-    )(meta, x_halo, x, dy, grad_lows, gain, shift, *triples, left, right, right, *outputs, output_left, output_left,
-      *tables)
+    )(meta, x_halo, normed, dy, grad_lows, gain, shift, *triples, left, right, right, *outputs, output_left,
+      output_left, *tables)
 
 
 def attend_rows(with_prev, start, count, q_ref, k_ref, v_ref, g_ref, kp_ref, vp_ref, tables, att_ref, gq_ref,
@@ -718,32 +882,69 @@
 
 
 def settle_kernel(
-    send_tiles, halo_start, tiles, per_device, meta_ref, normed_ref, low_ref, grad_lows_ref, out_in_ref,
-    att0_ref, att1_ref, gq0_ref, gq1_ref, gk0_ref, gk1_ref, gv0_ref, gv1_ref, halo0_ref, halo1_ref,
-    triple0_ref, triple1_ref, left_ref, output0_ref, output1_ref, right0_ref, right1_ref, output_left0_ref,
-    output_left1_ref, out_ref, send_ref, keep_ref, right_grad0_ref, right_grad1_ref, left_grad_ref,
-    output_left_grad0_ref, output_left_grad1_ref,
+    unit, tile, normed_ref, low_ref, grad_lows_ref, out_in_ref, att0_ref, att1_ref, gq0_ref, gq1_ref, gk0_ref, gk1_ref,
+    gv0_ref, gv1_ref, halo0_ref, halo1_ref, triple0_ref, triple1_ref, left_ref, output0_ref, output1_ref, right0_ref,
+    right1_ref, output_left0_ref, output_left1_ref, out_ref, keep_ref, right_grad0_ref, right_grad1_ref, left_grad_ref,
+    output_left_grad0_ref, output_left_grad1_ref, got_ref, send_ref, halo_got_ref, key_ref, value_ref, halo_sems, sems,
 ):
     step = pl.program_id(0)
-    here = (lax.rem(step + (meta_ref[PLACE] + 1) * per_device, tiles) >= halo_start).astype(F32)
+    per_device = got_ref.shape[1] // tile
+    steps = unit * per_device
+    halo_start = steps - SHORT // tile
+    place, base = place_in_unit(unit)
+    half = base // unit
+    peers = unit_peers(unit)
+    y_peer = chip_neighbours(unit)[1]
+    halo_copy = pltpu.make_async_remote_copy(
+        src_ref=halo1_ref, dst_ref=halo_got_ref, send_sem=halo_sems.at[0], recv_sem=halo_sems.at[1], device_id=y_peer,
+        device_id_type=MESH,
+    )
+    copies = [
+        [
+            pltpu.make_async_remote_copy(
+                src_ref=send_ref.at[s, pl.ds(t * tile, tile)], dst_ref=got_ref.at[s, pl.ds(t * tile, tile)],
+                send_sem=sems.at[0, s, t], recv_sem=sems.at[1, s, t], device_id=peer, device_id_type=MESH,
+            )
+            for t in range(per_device)
+        ]
+        for s, peer in enumerate(peers)
+    ]
+    sums = (right_grad0_ref, right_grad1_ref, left_grad_ref, output_left_grad0_ref, output_left_grad1_ref)
+
+    @pl.when(step == 0)
+    def _():
+        meet([y_peer, *peers])
+        pl.when(half == 1)(halo_copy.start)
+        for ref in sums:
+            ref[...] = jnp.zeros_like(ref)
+
+    key_ref[0], key_ref[1] = gk0_ref[...], gk1_ref[...]
+    value_ref[0], value_ref[1] = gv0_ref[...], gv1_ref[...]
+
+    @pl.when((half == 0) & (step >= halo_start))
+    def _():
+        pl.when(step == halo_start)(halo_copy.wait_recv)
+        span = pl.ds(pl.multiple_of((step - halo_start) * tile, tile), tile)
+        for shard, halo in enumerate((halo0_ref, halo_got_ref)):
+            key_ref[shard] = (key_ref[shard].astype(F32) + halo[0, span].astype(F32)).astype(BF16)
+            value_ref[shard] = (value_ref[shard].astype(F32) + halo[1, span].astype(F32)).astype(BF16)
+
     normed = normed_ref[...]
     low = low_ref[...]
     grad_low_out = grad_lows_ref[:, :LANES]
     att0, att1 = att0_ref[...], att1_ref[...]
     first = low_lanes()
 
-    def mixed(gq, gk, gv, halo):
-        key = (gk[...].astype(F32) + here * halo[0].astype(F32)).astype(BF16)
-        value = (gv[...].astype(F32) + here * halo[1].astype(F32)).astype(BF16)
-        query = gq[...]
+    def mixed(gq, shard):
+        query, key, value = gq[...], key_ref[shard], value_ref[shard]
         groups = []
         for start in range(0, query.shape[1], LANES):
             q, k, v = (part[:, start : start + LANES] for part in (query, key, value))
             groups += [jnp.where(first, q, k), jnp.where(first, v, q), jnp.where(first, k, v)]
         return jnp.concatenate(groups, axis=1)
 
-    grad0 = mixed(gq0_ref, gk0_ref, gv0_ref, halo0_ref)
-    grad1 = mixed(gq1_ref, gk1_ref, gv1_ref, halo1_ref)
+    grad0 = mixed(gq0_ref, 0)
+    grad1 = mixed(gq1_ref, 1)
     grad_low = (dot_nt(grad0, right0_ref[...]) + dot_nt(grad1, right1_ref[...])).astype(BF16)
     grad = (
         dot_nt(grad0, triple0_ref[...]) + dot_nt(grad1, triple1_ref[...]) + dot_nt(grad_low, left_ref[...])
@@ -752,18 +953,22 @@
     low_att = (dot_nn(att0, output_left0_ref[...]) + dot_nn(att1, output_left1_ref[...])).astype(BF16)
     width = grad.shape[1]
 
-    def put(ref):
-        ref[:, :width] = grad
-        ref[:, width:] = low_att
-
-    pl.when(step < send_tiles)(lambda: put(send_ref))
-    pl.when(step >= send_tiles)(lambda: put(keep_ref))
-    sums = (right_grad0_ref, right_grad1_ref, left_grad_ref, output_left_grad0_ref, output_left_grad1_ref)
-
-    @pl.when(step == 0)
-    def _():
-        for ref in sums:
-            ref[...] = jnp.zeros_like(ref)
+    @pl.when(step // per_device == place)
+    def _():
+        keep_ref[:, :width] = grad
+        keep_ref[:, width:] = low_att
+
+    span = pl.ds(pl.multiple_of(lax.rem(step, per_device) * tile, tile), tile)
+    for s in range(unit - 1):
+        owner = lax.rem(place + unit - (s + 1), unit)
+
+        @pl.when(step // per_device == owner)
+        def _():
+            send_ref[s, span, :width] = grad
+            send_ref[s, span, width:] = low_att
+
+        for t in range(per_device):
+            pl.when(step == owner * per_device + t)(copies[s][t].start)
 
     right_grad0_ref[...] += dot_tn(low, grad0)
     right_grad1_ref[...] += dot_tn(low, grad1)
@@ -771,126 +976,78 @@
     output_left_grad0_ref[...] += dot_tn(grad_low_out, att0)
     output_left_grad1_ref[...] += dot_tn(grad_low_out, att1)
 
-
-def settle(meta, normed, low, grad_lows, out, pairs, halos, triples, left, outputs, right, output_left, own_rows, tile):
+    @pl.when(step == steps - 1)
+    def _():
+        pl.when(half == 1)(halo_copy.wait_send)
+        for group in copies:
+            for copy in group:
+                copy.wait()
+
+
+def settle(unit, normed, low, grad_lows, out, pairs, halos, triples, left, outputs, right, output_left, tile):
     rows, width = normed.shape
+    own_rows = rows // unit
     head_width = pairs[0].shape[1]
-    send_rows = rows - own_rows
-    send_tiles, tiles, per_device = send_rows // tile, rows // tile, own_rows // tile
-    halo_start = (rows - SHORT) // tile
-    row_spec = functools.partial(ordered, tiles=tiles, per_device=per_device)
-
-    def halo_index(i, meta):
-        return (0, jnp.maximum(lax.rem(i + (meta[PLACE] + 1) * per_device, tiles) - halo_start, 0), 0)
+    steps, per_device = rows // tile, own_rows // tile
+    anywhere = pl.BlockSpec(memory_space=pl.ANY)
+
+    def own(i):
+        return lax.axis_index("mp")
+
+    def far(i):
+        return lax.rem(lax.axis_index("mp") + unit, 2 * unit)
+
+    def kept(i):
+        return (jnp.clip(i - place_in_unit(unit)[0] * per_device, 0, per_device - 1), 0)
 
     return pl.pallas_call(
-        functools.partial(settle_kernel, send_tiles, halo_start, tiles, per_device),
-        grid_spec=pltpu.PrefetchScalarGridSpec(
-            num_scalar_prefetch=1,
-            grid=(tiles,),
-            in_specs=[row_spec(tile, width), row_spec(tile, LANES), row_spec(tile, 2 * LANES), row_spec(tile, width)]
-            + [row_spec(tile, head_width)] * 8
-            + [pl.BlockSpec((2, tile, head_width), halo_index)] * 2
-            + [whole(value.shape) for value in (*triples, left, *outputs)]
-            + [at_columns((LANES, 3 * head_width), which) for which in (OWN, FAR)]
-            + [at_rows((head_width, LANES), which) for which in (OWN, FAR)],
-            out_specs=[
-                row_spec(tile, width),
-                sent(tile, width + LANES, send_tiles),
-                kept(tile, width + LANES, send_tiles),
-                held((LANES, 3 * head_width)),
-                held((LANES, 3 * head_width)),
-                held((LANES, width)),
-                held((LANES, head_width)),
-                held((LANES, head_width)),
-            ],
-        ),
+        functools.partial(settle_kernel, unit, tile),
+        grid=(steps,),
+        in_specs=[rows_of(tile, width), rows_of(tile, LANES), rows_of(tile, 2 * LANES), rows_of(tile, width)]
+        + [rows_of(tile, head_width)] * 8
+        + [whole(halos[0].shape), anywhere]
+        + [whole(value.shape) for value in (*triples, left, *outputs)]
+        + [
+            pl.BlockSpec((LANES, 3 * head_width), lambda i: (0, own(i)), pipeline_mode=pl.Buffered(1)),
+            pl.BlockSpec((LANES, 3 * head_width), lambda i: (0, far(i)), pipeline_mode=pl.Buffered(1)),
+            pl.BlockSpec((head_width, LANES), lambda i: (own(i), 0), pipeline_mode=pl.Buffered(1)),
+            pl.BlockSpec((head_width, LANES), lambda i: (far(i), 0), pipeline_mode=pl.Buffered(1)),
+        ],
+        out_specs=[
+            rows_of(tile, width),
+            pl.BlockSpec((tile, width + LANES), kept),
+            held((LANES, 3 * head_width)),
+            held((LANES, 3 * head_width)),
+            held((LANES, width)),
+            held((LANES, head_width)),
+            held((LANES, head_width)),
+            anywhere,
+        ],
+        scratch_shapes=[
+            pltpu.VMEM((unit - 1, own_rows, width + LANES), BF16),
+            pltpu.VMEM((2, SHORT, head_width), BF16),
+            pltpu.VMEM((2, tile, head_width), BF16),
+            pltpu.VMEM((2, tile, head_width), BF16),
+            pltpu.SemaphoreType.DMA((2,)),
+            pltpu.SemaphoreType.DMA((2, unit - 1, per_device)),
+        ],
         out_shape=[
             shaped((rows, width), F32),
-            shaped((send_rows, width + LANES), BF16),
             shaped((own_rows, width + LANES), BF16),
             shaped((LANES, 3 * head_width), F32),
             shaped((LANES, 3 * head_width), F32),
             shaped((LANES, width), F32),
             shaped((LANES, head_width), F32),
             shaped((LANES, head_width), F32),
+            shaped((unit - 1, own_rows, width + LANES), BF16),
         ],
-        compiler_params=params(),
+        compiler_params=pltpu.CompilerParams(
+            dimension_semantics=("arbitrary",), vmem_limit_bytes=VMEM_LIMIT, collective_id=5, has_side_effects=True
+        ),
         cost_estimate=BRIEF,
         name="settle",
-    )(meta, normed, low, grad_lows, out, *pairs, *halos, *triples, left, *outputs, right, right, output_left,
+    )(normed, low, grad_lows, out, *pairs, *halos, *triples, left, *outputs, right, right, output_left,
       output_left)
-
-
-def finish_kernel(
-    parts, x_ref, dy_ref, gain1_ref, gain2_ref, output_right_ref, shrink_right_ref, *refs
-):
-    attention, feed = refs[:parts], refs[parts : 2 * parts]
-    y_ref, dx_ref, norms_ref, output_right_grad_ref, shrink_right_grad_ref = refs[2 * parts :]
-    width = x_ref.shape[1]
-
-    def total(values, start, size):
-        value = values[0][:, start : start + size].astype(F32)
-        for other in values[1:]:
-            value = value + other[:, start : start + size].astype(F32)
-        return value
-
-    out = total(feed, 0, width)
-    first = total(attention, 0, width)
-    second = total(feed, width, width)
-    low_att = total(attention, width, LANES).astype(BF16)
-    low_act = total(feed, 2 * width, LANES).astype(BF16)
-    x = x_ref[...].astype(F32)
-    dy = dy_ref[...]
-    y_ref[...] = (
-        x + out + dot_nn(low_att, output_right_ref[...]) + dot_nn(low_act, shrink_right_ref[...])
-    ).astype(BF16)
-    center = x - jnp.mean(x, axis=-1, keepdims=True)
-    spread = jnp.mean(center * center, axis=-1, keepdims=True)
-    inverse = lax.rsqrt(spread + EPS)
-    unit = center * inverse
-    scaled = first * gain1_ref[...] + second * gain2_ref[...]
-    mean = jnp.mean(scaled, axis=-1, keepdims=True)
-    inner = jnp.mean(scaled * unit, axis=-1, keepdims=True)
-    dx_ref[...] = dy.astype(F32) + (scaled - mean - unit * inner) * inverse
-
-    @pl.when(pl.program_id(0) == 0)
-    def _():
-        norms_ref[...] = jnp.zeros_like(norms_ref)
-        output_right_grad_ref[...] = jnp.zeros_like(output_right_grad_ref)
-        shrink_right_grad_ref[...] = jnp.zeros_like(shrink_right_grad_ref)
-
-    norms_ref[0:1, :] += jnp.sum(first * unit, axis=0, keepdims=True)
-    norms_ref[1:2, :] += jnp.sum(first, axis=0, keepdims=True)
-    norms_ref[2:3, :] += jnp.sum(second * unit, axis=0, keepdims=True)
-    norms_ref[3:4, :] += jnp.sum(second, axis=0, keepdims=True)
-    output_right_grad_ref[...] += dot_tn(low_att, dy)
-    shrink_right_grad_ref[...] += dot_tn(low_act, dy)
-
-
-def finish(x, dy, gain1, gain2, output_right, shrink_right, attention, feed, tile):
-    rows, width = x.shape
-    parts = len(attention)
-    return pl.pallas_call(
-        functools.partial(finish_kernel, parts),
-        grid=(rows // tile,),
-        in_specs=[rows_of(tile, width)] * 2
-        + [whole((1, width))] * 2
-        + [whole(output_right.shape)] * 2
-        + [rows_of(tile, width + LANES)] * parts
-        + [rows_of(tile, 2 * width + LANES)] * parts,
-        out_specs=[rows_of(tile, width)] * 2 + [held((8, width)), held((LANES, width)), held((LANES, width))],
-        out_shape=[
-            shaped((rows, width), BF16),
-            shaped((rows, width), F32),
-            shaped((8, width), F32),
-            shaped((LANES, width), F32),
-            shaped((LANES, width), F32),
-        ],
-        compiler_params=params(),
-        cost_estimate=BRIEF,
-        name="finish",
-    )(x, dy, gain1, gain2, output_right, shrink_right, *attention, *feed)
 
 
 SUM_ROWS = (2, 4, 16)
@@ -1146,60 +1303,36 @@
     gain1, shift1 = first_gain[None, :], first_shift[None, :]
     gain2, shift2 = second_gain[None, :], second_shift[None, :]
 
-    x, dy = unit_gather(unit, block_input, cotangent)
-    x_halo = lax.ppermute(x[rows - SHORT :], "mp", onward)
-
-    def over_y(matrix):
-        count = matrix.shape[0] // 2
-        return lax.ppermute(lax.dynamic_slice_in_dim(matrix, lead * count, count, 0), "mp", swap)
-
-    def over_x(piece):
-        return lax.ppermute(piece, "dp", beside)
-
-    (normed2, low2, grad_lows, out, grad2, low_act, grad_low2, expand_right_own, shrink_left_own, triple_far,
-     output_far) = feed_first(
-        unit, x, dy, gain2, shift2, expand_weight, expand_left, expand_right, shrink_weight, shrink_left, output_right,
-        shrink_right, triple_weight, output_weight, tile,
-    )
-    expand_weight_late, shrink_weight_late, grad_lows = lax.optimization_barrier(
-        (expand_weight, shrink_weight, grad_lows)
-    )
-    expand_piece = over_y(expand_weight_late)
-    shrink_piece = over_y(shrink_weight_late)
-    normed1, low1, q, k, v, g = project(
-        meta, x_halo, x, dy, grad_lows, gain1, shift1, (triple_weight, triple_far), triple_left, triple_right,
+    (normed1, normed2, dy, low2, grad_lows, out, grad2, low_act, grad_low2, expand_right_own, shrink_left_own,
+     triple_far, output_far, x_halo, expand_half, shrink_half) = feed_first(
+        unit, block_input, cotangent, (gain1, shift1, gain2, shift2), expand_weight, expand_left, expand_right,
+        shrink_weight, shrink_left, output_right, shrink_right, triple_weight, output_weight, tile,
+    )
+    expand_piece = lax.ppermute(expand_half, "mp", swap)
+    shrink_piece = lax.ppermute(shrink_half, "mp", swap)
+    low1, q, k, v, g = project(
+        meta, x_halo, normed1, dy, grad_lows, gain1, shift1, (triple_weight, triple_far), triple_left, triple_right,
         (output_weight, output_far), output_left, tables, tile,
     )
+    expand_piece, q = lax.optimization_barrier((expand_piece, q))
+    expand_other = lax.ppermute(expand_piece, "dp", beside)
     count = 256
     att_far, gq_far, gk_far, gv_far, halo = attend(1, meta, q, k, v, g, tables, count)
     halo_own = lax.ppermute(halo, "mp", back)
-    expand_piece, q = lax.optimization_barrier((expand_piece, q))
-    expand_other = over_x(expand_piece)
+    shrink_piece, q = lax.optimization_barrier((shrink_piece, q))
+    shrink_other = lax.ppermute(shrink_piece, "dp", beside)
     att_own, gq_own, gk_own, gv_own, halo = attend(0, meta, q, k, v, g, tables, count)
-    halo_far = lax.ppermute(halo, "mp", back)
-    shrink_piece, att_own = lax.optimization_barrier((shrink_piece, att_own))
-    shrink_other = over_x(shrink_piece)
-    (out, send1, keep1, triple_right_own, triple_right_far, triple_left_sum, output_left_sum_own,
-     output_left_sum_far) = settle(
-        meta, normed1, low1, grad_lows, out,
-        (att_own, att_far, gq_own, gq_far, gk_own, gk_far, gv_own, gv_far), (halo_own, halo_far),
-        (triple_weight, triple_far), triple_left, (output_weight, output_far), triple_right, output_left, own_rows, tile,
-    )
-    send2, keep2, expand_right_far, shrink_left_far, expand_left_sum = feed_second(
-        meta, normed2, low2, dy, grad_lows, out, grad2, low_act, grad_low2, (expand_piece, expand_other), expand_left,
-        expand_right, (shrink_piece, shrink_other), shrink_left, own_rows, tile,
-    )
-
-    def pass_on(sent_rows):
-        got = []
-        for j in range(1, unit):
-            ring = [(m, m - m % unit + (m % unit + j) % unit) for m in range(ranks)]
-            got.append(lax.ppermute(sent_rows[(j - 1) * own_rows : j * own_rows], "mp", ring))
-        return got
-
-    block_output, input_gradient, norms, output_right_sum, shrink_right_sum = finish(
-        block_input, cotangent, gain1, gain2, output_right, shrink_right, [keep1] + pass_on(send1),
-        [keep2] + pass_on(send2), math.gcd(own_rows, 128),
+    (out, keep1, triple_right_own, triple_right_far, triple_left_sum, output_left_sum_own, output_left_sum_far,
+     got1) = settle(
+        unit, normed1, low1, grad_lows, out,
+        (att_own, att_far, gq_own, gq_far, gk_own, gk_far, gv_own, gv_far), (halo_own, halo),
+        (triple_weight, triple_far), triple_left, (output_weight, output_far), triple_right, output_left, tile,
+    )
+    (block_output, input_gradient, norms, output_right_sum, shrink_right_sum, expand_right_far, shrink_left_far,
+     expand_left_sum) = feed_second(
+        unit, normed2, low2, dy, grad_lows, out, grad2, low_act, grad_low2, block_input, keep1, got1, (gain1, gain2),
+        output_right, shrink_right, (expand_piece, expand_other), expand_left, expand_right,
+        (shrink_piece, shrink_other), shrink_left, tile,
     )
 
     own_sums = (triple_right_own, output_left_sum_own, expand_right_own, shrink_left_own)

time: 332 us -> 276 us (0.83)
  waiting for transfers between devices: 26.6 us -> 1.67 us
  Pallas kernels: 261 us -> 244 us
  starting transfers between devices: 23.1 us -> 8.1 us
  local copies, waits for them, and re-layouts: 14.3 us -> 10.5 us
    ppermute x8 -> x4, starting transfers between devices: 21.8 us -> 6.81 us  [the longest x1 3.47 us: shards(): expand_piece = lax.ppermute(expand_half, 'mp', swap)]
    ppermute x8 -> x4, waiting for transfers between devices: 15.8 us -> 1.66 us  [the longest x1 1.55 us: shards(): shrink_piece = lax.ppermute(shrink_half, 'mp', swap)]
    ppermute x1, waiting for transfers between devices: 10.9 us -> 0.01 us  [shards(): halo_own = lax.ppermute(halo, 'mp', back)]
    pallas_call x6 -> x4, Pallas kernels: 140 us -> 132 us  [the longest x1 42.6 us: feed_first(): pl.pallas_call(functools.partial(feed_first_kernel, unit, tile), grid=(st...]
    pallas_call x2, Pallas kernels: 45.8 us -> 39.1 us  [attend(): pl.pallas_call(functools.partial(attend_kernel, blocks, count), grid_spec...]
    unnamed x52 -> x38, local copies, waits for them, and re-layouts: 7.71 us -> 7.35 us
  transfers between devices with their start and end apart: 9 -> 5, of which waited for: 4 -> 2; matrix products, arithmetic and copies ran while one was open for 1% -> 2% of each run, Pallas kernels for 42% -> 34%
where the time goes in v1:
time: 276 us; the launch traced here: 273 us
  Pallas kernels  244 us (88%)
  local copies, waits for them, and re-layouts  10.5 us (4%)
  starting transfers between devices  8.1 us (3%)
  other arithmetic  7.23 us (3%)
    pallas_call x1, Pallas kernels, sum_all(): pl.pallas_call(functools.partial(sum_kernel, chunks, width, extra), out_s...  67.5 us
    pallas_call x1, Pallas kernels, feed_first(): pl.pallas_call(functools.partial(feed_first_kernel, unit, tile), grid=(st...  42.6 us
    pallas_call x2, Pallas kernels, attend(): pl.pallas_call(functools.partial(attend_kernel, blocks, count), grid_spec...  39.1 us
    pallas_call x1, Pallas kernels, feed_second(): pl.pallas_call(functools.partial(feed_second_kernel, unit, tile), grid=(s...  34.5 us
    pallas_call x1, Pallas kernels, settle(): pl.pallas_call(functools.partial(settle_kernel, unit, tile), grid=(steps,...  32.5 us
    pallas_call x1, Pallas kernels, project(): pl.pallas_call(functools.partial(project_kernel, main_tiles), grid_spec=p...  22.2 us
    unnamed x38, local copies, waits for them, and re-layouts  7.35 us
    pallas_call x1, Pallas kernels, unpack(): pl.pallas_call(functools.partial(unpack_kernel, (triple_width, head_width...  5.98 us
  transfers between devices with their start and end apart: 5, of which 2 were waited for; matrix products, arithmetic and copies ran while one was open for 2% of the time, Pallas kernels for 34%

profile of v1, /device:TPU:1, one launch (start us, length us, event | category | flops | bytes accessed | tf_op | source)
XLA Modules:
  0.0 272.9 jit_solution(9446234417299553302)
XLA Ops:
  0.7 42.6 %feed_first.1 = (bf16[1536,1024]{1,0:T(8,128)(2,1)}, bf16[1536,1024]{1,0:T(8,128)(2,1)}, bf16[1536,1024]{1,0:T(8,128)(2,1)}, bf16[1536,128]{1,0:T(8,128)(2,1)}, ...) custom-call(bf16[768,1024]{1,0:T(8,128)(2,1)} %x_ref.3, ...), custom_call_target="tpu_custom_call" | custom-call | flops 1 | bytes 1 | tf_op jit(solution)/shard_map/feed_first/pallas_call | solution.py:378
  43.2 3.5 %collective-permute-start.1 = (bf16[512,1024]{1,0:T(8,128)(2,1)}, bf16[512,1024]{1,0:T(8,128)(2,1)S(1)}, u32[]{:S(2)}, u32[]{:S(2)}) collective-permute-start(bf16[512,1024]{1,0:T(8,128)(2,1)} %get-tuple-element.87), channel_id=1, source_target_pairs={{0,2},{1,3},{2,0},{3,1},{4,6},{5,7},{6,4},{7,5},{8,10},{9,11},{10,... | collective-permute-start | bytes 3145736 | tf_op jit(solution)/shard_map/ppermute | solution.py:1311
  47.9 22.2 %project.1 = (bf16[1536,128]{1,0:T(8,128)(2,1)}, bf16[1536,512]{1,0:T(8,128)(2,1)}, bf16[2048,512]{1,0:T(8,128)(2,1)}, bf16[2048,512]{1,0:T(8,128)(2,1)}, bf16[1536,512]{1,0:T(8,128)(2,1)}) custom-call(s32[7]{0:T(128)} %concatenate.13.meta_ref, bf16[512,1024]{1,0:T(8,128)(2,1)} %get-tuple-element.81.x_halo_ref, ...), custom_call_target="tpu_custom_call" | custom-call | flops 1 | bytes 1 | tf_op jit(solution)/shard_map/project/pallas_call | solution.py:714
  70.2 19.6 %attend.3 = (bf16[1536,256]{1,0:T(8,128)(2,1)}, bf16[1536,256]{1,0:T(8,128)(2,1)}, bf16[1536,256]{1,0:T(8,128)(2,1)}, bf16[1536,256]{1,0:T(8,128)(2,1)}, bf16[2,512,256]{2,1,0:T(8,128)(2,1)}) custom-call(s32[7]{0:T(128)} %concatenate.13.meta_ref, bf16[1536,512]{1,0:T(8,128)(2,1)} %get-tuple-element.90.q_ref, ...), custom_call_target="tpu_custom_call" | custom-call | flops 1 | bytes 1 | tf_op jit(solution)/shard_map/attend/pallas_call | solution.py:868
  89.8 1.3 collective-permute-start.2
  91.1 1.5 collective-permute-done.down0_ref
  92.6 3.2 %collective-permute-start.4 = (bf16[512,1024]{1,0:T(8,128)(2,1)S(1)}, bf16[512,1024]{1,0:T(8,128)(2,1)S(1)}, u32[]{:S(2)}, u32[]{:S(2)}) collective-permute-start(bf16[512,1024]{1,0:T(8,128)(2,1)S(1)} %collective-permute-done.down0_ref), channel_id=1, source_target_pairs={{0,4},{4,0},{8,12},{12,8},{16,20},{20,16},{24,28},{28,24},{1,5},{5... | collective-permute-start | bytes 3145736 | tf_op jit(solution)/shard_map/ppermute | solution.py:1323
  96.0 19.5 %attend.2 = (bf16[1536,256]{1,0:T(8,128)(2,1)}, bf16[1536,256]{1,0:T(8,128)(2,1)}, bf16[1536,256]{1,0:T(8,128)(2,1)}, bf16[1536,256]{1,0:T(8,128)(2,1)}, bf16[2,512,256]{2,1,0:T(8,128)(2,1)}) custom-call(s32[7]{0:T(128)} %concatenate.13.meta_ref, bf16[1536,512]{1,0:T(8,128)(2,1)} %get-tuple-element.90.q_ref, ...), custom_call_target="tpu_custom_call" | custom-call | flops 1 | bytes 1 | tf_op jit(solution)/shard_map/attend/pallas_call | solution.py:868
  116.3 32.5 %settle.1 = (f32[1536,1024]{1,0:T(8,128)}, bf16[768,1152]{1,0:T(8,128)(2,1)}, f32[128,768]{1,0:T(8,128)}, f32[128,768]{1,0:T(8,128)}, f32[128,1024]{1,0:T(8,128)...) custom-call(bf16[1536,1024]{1,0:T(8,128)(2,1)} %get-tuple-element.80.normed_ref, ...), custom_call_target="tpu_custom_call" | custom-call | flops 1 | bytes 1 | tf_op jit(solution)/shard_map/settle/pallas_call | solution.py:1003
  148.8 1.1 convert_element_type.47
  150.0 1.0 convert_element_type.39
  151.0 0.9 convert_element_type.40
  152.1 0.9 copy-done.4
  153.4 34.5 %feed_second.1 = (bf16[768,1024]{1,0:T(8,128)(2,1)}, f32[768,1024]{1,0:T(8,128)}, f32[8,1024]{1,0:T(8,128)}, f32[128,1024]{1,0:T(8,128)}, f32[128,1024]{1,0:T(8,...) custom-call(bf16[1536,1024]{1,0:T(8,128)(2,1)} %get-tuple-element.76.normed_ref, ...), custom_call_target="tpu_custom_call" | custom-call | flops 1 | bytes 1 | tf_op jit(solution)/shard_map/feed_second/pallas_call | solution.py:583
  187.9 1.1 convert_element_type.48
  189.0 1.1 convert_element_type.49
  191.1 1.1 copy.46
  192.6 1.3 pad_maximum_fusion.part_ref
  193.9 67.5 %sum_all.1 = (bf16[2,2,2,4,16,3072]{5,4,3,2,1,0:T(8,128)(2,1)}, bf16[2,2,2,4,16,1152]{5,4,3,2,1,0:T(8,128)(2,1)}) custom-call(bf16[2,2,4,16,3072]{4,3,2,1,0:T(8,128)(2,1)} %pad_maximum_fusion.part_ref, bf16[2,2,2,4,16,1152]{5,4,3,2,1,0:T(8,128)(2,1)} %bitcast.69), custom_call_target="tpu_custom_call" | custom-call | flops 1 | bytes 1 | tf_op jit(solution)/shard_map/sum_all/pallas_call | solution.py:1181
  261.4 6.0 %unpack.1 = (f32[128,3072]{1,0:T(8,128)}, f32[1024,128]{1,0:T(8,128)}, f32[128,4096]{1,0:T(8,128)}, f32[4096,128]{1,0:T(8,128)}, f32[1024,128]{1,0:T(8,128)}, /*...) custom-call(bf16[2,2,128,3072]{3,2,1,0:T(8,128)(2,1)} %bitcast.70, ...), custom_call_target="tpu_custom_call" | custom-call | flops 1 | bytes 1 | tf_op jit(solution)/shard_map/unpack/pallas_call | solution.py:1232
  267.4 1.3 slice_bitcast_fusion
  268.8 1.1 copy.64
  269.9 1.3 copy-done
  271.2 1.7 copy.65
  (58 shorter events, 4.0 us)
Async XLA Ops:
  0.6 46.2 %copy-start.14 = (s32[1,6]{1,0:T(1,128)S(1)}, s32[1,6]{1,0:T(1,128)}, u32[]{:S(2)}) copy-start(s32[1,6]{1,0:T(1,128)} %param.23) | copy-start | bytes 76
  43.2 26.9 %collective-permute-start.1 = (bf16[512,1024]{1,0:T(8,128)(2,1)}, bf16[512,1024]{1,0:T(8,128)(2,1)S(1)}, u32[]{:S(2)}, u32[]{:S(2)}) collective-permute-start(bf16[512,1024]{1,0:T(8,128)(2,1)} %get-tuple-element.87), channel_id=1, source_target_pairs={{0,2},{1,3},{2,0},{3,1},{4,6},{5,7},{6,4},{7,5},{8,10},{9,11},{10,... | collective-permute-start | bytes 3145736 | tf_op jit(solution)/shard_map/ppermute | solution.py:1311
  46.7 45.9 %collective-permute-start = (bf16[512,1024]{1,0:T(8,128)(2,1)}, bf16[512,1024]{1,0:T(8,128)(2,1)S(1)}, u32[]{:S(2)}, u32[]{:S(2)}) collective-permute-start(bf16[512,1024]{1,0:T(8,128)(2,1)} %get-tuple-element.86), channel_id=1, source_target_pairs={{0,2},{1,3},{2,0},{3,1},{4,6},{5,7},{6,4},{7,5},{8,10},{9,11},{10,... | collective-permute-start | bytes 3145736 | tf_op jit(solution)/shard_map/ppermute | solution.py:1312
  70.2 25.6 %copy-start.2 = (bf16[512,1024]{1,0:T(8,128)(2,1)}, bf16[512,1024]{1,0:T(8,128)(2,1)S(1)}, u32[]{:S(2)}) copy-start(bf16[512,1024]{1,0:T(8,128)(2,1)S(1)} %collective-permute-done.1.up0_ref) | copy-start | bytes 3145732
  70.2 25.7 %copy-start.8 = (f32[128,1024]{1,0:T(8,128)S(1)}, f32[128,1024]{1,0:T(8,128)}, u32[]{:S(2)}) copy-start(f32[128,1024]{1,0:T(8,128)} %get-tuple-element.116) | copy-start | bytes 1572868
  70.2 25.8 %copy-start.7 = (f32[128,1024]{1,0:T(8,128)S(1)}, f32[128,1024]{1,0:T(8,128)}, u32[]{:S(2)}) copy-start(f32[128,1024]{1,0:T(8,128)} %get-tuple-element.117) | copy-start | bytes 1572868
  89.8 25.7 %collective-permute-start.2 = (bf16[2,512,256]{2,1,0:T(8,128)(2,1)}, bf16[2,512,256]{2,1,0:T(8,128)(2,1)S(1)}, u32[]{:S(2)}, u32[]{:S(2)}) collective-permute-start(bf16[2,512,256]{2,1,0:T(8,128)(2,1)} %get-tuple-element.102), channel_id=1, source_target_pairs={{2,0},{3,1},{6,4},{7,5},{10,8},{11,9},{14,12},{15,13},{18,16},{19,... | collective-permute-start | bytes 1572872 | tf_op jit(solution)/shard_map/ppermute | solution.py:1321
  92.6 22.8 %copy-start.3 = (bf16[512,1024]{1,0:T(8,128)(2,1)}, bf16[512,1024]{1,0:T(8,128)(2,1)S(1)}, u32[]{:S(2)}) copy-start(bf16[512,1024]{1,0:T(8,128)(2,1)S(1)} %collective-permute-done.down0_ref) | copy-start | bytes 3145732
  92.6 59.4 %collective-permute-start.4 = (bf16[512,1024]{1,0:T(8,128)(2,1)S(1)}, bf16[512,1024]{1,0:T(8,128)(2,1)S(1)}, u32[]{:S(2)}, u32[]{:S(2)}) collective-permute-start(bf16[512,1024]{1,0:T(8,128)(2,1)S(1)} %collective-permute-done.down0_ref), channel_id=1, source_target_pairs={{0,4},{4,0},{8,12},{12,8},{16,20},{20,16},{24,28},{28,24},{1,5},{5... | collective-permute-start | bytes 3145736 | tf_op jit(solution)/shard_map/ppermute | solution.py:1323
  95.8 56.3 %collective-permute-start.3 = (bf16[512,1024]{1,0:T(8,128)(2,1)S(1)}, bf16[512,1024]{1,0:T(8,128)(2,1)S(1)}, u32[]{:S(2)}, u32[]{:S(2)}) collective-permute-start(bf16[512,1024]{1,0:T(8,128)(2,1)S(1)} %collective-permute-done.1.up0_ref), channel_id=1, source_target_pairs={{0,4},{4,0},{8,12},{12,8},{16,20},{20,16},{24,28},{28,24},{1,5},{5... | collective-permute-start | bytes 3145736 | tf_op jit(solution)/shard_map/ppermute | solution.py:1318
  115.5 0.8 copy-start.6
  148.8 3.1 %copy-start.12 = (f32[128,768]{1,0:T(8,128)S(1)}, f32[128,768]{1,0:T(8,128)}, u32[]{:S(2)}) copy-start(f32[128,768]{1,0:T(8,128)} %get-tuple-element.118) | copy-start | bytes 1179652
  148.8 3.1 %copy-start.13 = (f32[128,256]{1,0:T(8,128)S(1)}, f32[128,256]{1,0:T(8,128)}, u32[]{:S(2)}) copy-start(f32[128,256]{1,0:T(8,128)} %get-tuple-element.119) | copy-start | bytes 393220
  152.1 1.0 copy-start.4
  152.1 1.3 copy-start.5
  187.9 2.2 copy-start.11
  191.0 1.2 copy-start.10
  191.1 1.4 copy-start.9
  261.4 7.3 %copy-start.1 = (bf16[768,1024]{1,0:T(8,128)(2,1)S(1)}, bf16[768,1024]{1,0:T(8,128)(2,1)}, u32[]{:S(2)}) copy-start(bf16[768,1024]{1,0:T(8,128)(2,1)} %get-tuple-element.156) | copy-start | bytes 4718596
  268.8 2.5 copy-start
